TPU v7x, 128 devices: a whole 4x4x4 slice. The times are simulated.
128 devices in a mesh: seq: 32 (over y, z, core), head: 4 (over x).
Axes of the slice: x: 4, y: 4, z: 4, core: 2. Of those that a mesh axis runs over, the one named last changes fastest.
Arguments:
- hidden: bfloat16 [8192, 2048], P('seq'), may hold values from -45 to 45, as said below
- w_query: bfloat16 [2048, 2048], P(None, 'head'), may hold values from -0.125 to 0.125
- w_key: bfloat16 [2048, 2048], P(None, 'head'), may hold values from -0.125 to 0.125
- w_value: bfloat16 [2048, 4096], P(None, 'head'), may hold values from -0.125 to 0.125
- w_gate_z: bfloat16 [2048, 4096], P(None, 'head'), may hold values from -0.125 to 0.125
- w_decay: bfloat16 [2048, 32], P(None, 'head'), may hold values from -0.125 to 0.125
- w_beta: bfloat16 [2048, 32], P(None, 'head'), may hold values from -0.125 to 0.125
- conv_query: bfloat16 [4, 2048], P(None, 'head'), may hold values from -3 to 3
- conv_key: bfloat16 [4, 2048], P(None, 'head'), may hold values from -3 to 3
- conv_value: bfloat16 [4, 4096], P(None, 'head'), may hold values from -3 to 3
- decay_log: float32 [32], P('head'), may hold values from -3.6 to -0.69
- decay_bias: float32 [32], P('head'), may hold values from -13 to 0.5
- beta_bias: float32 [32], P('head'), may hold values from -5.5 to 1
- norm_gain: float32 [128], replicated, may hold values from 0.5 to 1.5
- w_out: bfloat16 [4096, 2048], P('head'), may hold values from -0.09375 to 0.09375
- state_in: float32 [32, 128, 128], P('head'), may hold values from -0.6 to 0.6
Outputs:
- mixed: bfloat16 [8192, 2048], P(('seq', 'head'))
Inputs may be any that keep to these rules, and one draw needn't show every extreme that they name: `hidden`: activations of order one with a few rows of ten times that size.
All inputs are finite; a program needn't handle non-finite values.
Results may differ from a plain program's by a relative error of at most 0.0062.
Values may be sent and summed in bfloat16 or wider, within the bound.
A program may use at most 128 MiB of HBM per device.

v0:
```python
import jax
import jax.numpy as jnp
from jax import lax
from jax.sharding import PartitionSpec as P

DK = 128
DV = 128


def passed_along(block, axis, distance):
    devices = range(lax.axis_size(axis))
    route = [(i - distance, i) for i in devices if i - distance in devices]
    return lax.ppermute(block, axis, route)


def unit_rows(values):
    return values * lax.rsqrt(jnp.sum(values * values, axis=-1, keepdims=True) + 1e-06)


def to_blocks(values, count, block):
    heads = values.shape[1]
    return values.reshape(count, block, heads, values.shape[2]).transpose(0, 2, 1, 3)


def on_device(
    hidden,
    w_query,
    w_key,
    w_value,
    w_gate_z,
    w_decay,
    w_beta,
    conv_query,
    conv_key,
    conv_value,
    decay_log,
    decay_bias,
    beta_bias,
    norm_gain,
    w_out,
    state_in,
):
    peak_magnitude = lax.Precision.HIGHEST
    rows = hidden.shape[0]
    heads_v = decay_log.shape[0]
    heads_k = w_query.shape[1] // DK
    width_q = w_query.shape[1]
    width_k = w_key.shape[1]
    query_raw = jnp.dot(hidden, w_query, preferred_element_type=jnp.float32).astype(jnp.bfloat16)
    key_raw = jnp.dot(hidden, w_key, preferred_element_type=jnp.float32).astype(jnp.bfloat16)
    value_raw = jnp.dot(hidden, w_value, preferred_element_type=jnp.float32).astype(jnp.bfloat16)
    raw_all = jnp.concatenate([query_raw, key_raw, value_raw], 1)
    margin = conv_query.shape[0] - 1
    earlier = passed_along(raw_all[rows - margin :], "seq", 1)
    padded = jnp.concatenate([earlier, raw_all], 0)
    taps_all = jnp.concatenate([conv_query, conv_key, conv_value], 1).astype(jnp.float32)
    summed = jnp.zeros(raw_all.shape, jnp.float32)
    for tap in range(margin + 1):
        summed = summed + taps_all[tap] * padded[tap : tap + rows].astype(jnp.float32)
    acted = jax.nn.silu(summed)
    query = unit_rows(acted[:, :width_q].reshape(rows, heads_k, DK)) * DK ** (-0.5)
    keys = unit_rows(acted[:, width_q : width_q + width_k].reshape(rows, heads_k, DK))
    values = acted[:, width_q + width_k :].reshape(rows, heads_v, DV)
    gate_log = -jnp.exp(decay_log) * jax.nn.softplus(
        jnp.dot(hidden, w_decay, preferred_element_type=jnp.float32) + decay_bias
    )
    strength = jax.nn.sigmoid(
        jnp.dot(hidden, w_beta, preferred_element_type=jnp.float32) + beta_bias
    )
    gate_z = jnp.dot(hidden, w_gate_z, preferred_element_type=jnp.float32)
    repeat_count = heads_v // heads_k
    query = jnp.repeat(query, repeat_count, axis=1)
    keys = jnp.repeat(keys, repeat_count, axis=1)
    block = min(64, rows)
    count = rows // block
    query_b = to_blocks(query, count, block)
    keys_b = to_blocks(keys, count, block)
    values_b = to_blocks(values, count, block)
    gate_b = gate_log.reshape(count, block, heads_v).transpose(0, 2, 1)
    strength_b = strength.reshape(count, block, heads_v).transpose(0, 2, 1)
    cumul = jnp.cumsum(gate_b, axis=-1)
    positions = jnp.arange(block)
    lower_incl = positions[:, None] >= positions[None, :]
    strict = positions[:, None] > positions[None, :]
    spread = cumul[..., :, None] - cumul[..., None, :]
    ratio_mat = jnp.where(lower_incl, jnp.exp(jnp.where(lower_incl, spread, 0.0)), 0.0)
    key_key = jnp.einsum("nhtd,nhjd->nhtj", keys_b, keys_b, precision=peak_magnitude)
    query_key = jnp.einsum("nhtd,nhjd->nhtj", query_b, keys_b, precision=peak_magnitude)
    lower_part = jnp.where(strict, strength_b[..., :, None] * ratio_mat * key_key, 0.0)
    system = lower_part + jnp.eye(block, dtype=jnp.float32)
    scale_now = jnp.exp(cumul)
    rhs = jnp.concatenate(
        [strength_b[..., None] * values_b, (strength_b * scale_now)[..., None] * keys_b], -1
    )
    solved = lax.linalg.triangular_solve(
        system, rhs, left_side=True, lower=True, unit_diagonal=True
    )
    corrected = solved[..., :DV]
    weights_key = solved[..., DV:]
    attend = query_key * ratio_mat
    local_out = jnp.einsum("nhtj,nhjv->nhtv", attend, corrected, precision=peak_magnitude)
    query_eff = scale_now[..., None] * query_b - jnp.einsum(
        "nhtj,nhjd->nhtd", attend, weights_key, precision=peak_magnitude
    )
    key_tail = jnp.exp(cumul[..., -1:] - cumul)[..., None] * keys_b
    eye_key = jnp.eye(DK, dtype=jnp.float32)
    transition = jnp.exp(cumul[..., -1])[..., None, None] * eye_key - jnp.einsum(
        "nhtd,nhte->nhde", key_tail, weights_key, precision=peak_magnitude
    )
    inject = jnp.einsum("nhtd,nhtv->nhdv", key_tail, corrected, precision=peak_magnitude)

    def advance(carry, piece):
        running_state, transform = carry
        loc, qeff, trans, inj = piece
        layer_output = loc + jnp.einsum(
            "htd,hdv->htv", qeff, running_state, precision=peak_magnitude
        )
        reach = jnp.einsum("htd,hde->hte", qeff, transform, precision=peak_magnitude)
        running_state = (
            jnp.einsum("hde,hev->hdv", trans, running_state, precision=peak_magnitude) + inj
        )
        transform = jnp.einsum("hde,hef->hdf", trans, transform, precision=peak_magnitude)
        return ((running_state, transform), (layer_output, reach))

    eye_heads = jnp.broadcast_to(eye_key, (heads_v, DK, DK))
    zero_state = jnp.zeros((heads_v, DK, DV), jnp.float32)
    pieces = (local_out, query_eff, transition, inject)
    (local_state, local_map), (outs, reaches) = lax.scan(advance, (zero_state, eye_heads), pieces)
    position = lax.axis_index("seq")

    def relay(step, incoming):
        leaving = (
            jnp.einsum("hde,hev->hdv", local_map, incoming, precision=peak_magnitude) + local_state
        )
        arrived = passed_along(leaving, "seq", 1)
        return jnp.where(position == 0, state_in, arrived)

    entering = lax.fori_loop(0, lax.axis_size("seq") - 1, relay, state_in)
    final_pair, (blocks_out, spare) = lax.scan(advance, (entering, eye_heads), pieces)
    core = blocks_out.transpose(0, 2, 1, 3).reshape(rows, heads_v, DV)
    scale = lax.rsqrt(jnp.mean(core * core, axis=-1, keepdims=True) + 1e-06)
    normed = (
        (core * scale * norm_gain * jax.nn.silu(gate_z.reshape(rows, heads_v, DV)))
        .astype(jnp.bfloat16)
        .reshape(rows, heads_v * DV)
    )
    result = lax.psum_scatter(
        jnp.dot(normed, w_out, preferred_element_type=jnp.float32),
        "head",
        scatter_dimension=0,
        tiled=True,
    )
    return result.astype(jnp.bfloat16)


def solution(mesh):
    placed = (
        P("seq", None),
        P(None, "head"),
        P(None, "head"),
        P(None, "head"),
        P(None, "head"),
        P(None, "head"),
        P(None, "head"),
        P(None, "head"),
        P(None, "head"),
        P(None, "head"),
        P("head"),
        P("head"),
        P("head"),
        P(),
        P("head", None),
        P("head", None, None),
    )
    return jax.shard_map(
        on_device, mesh=mesh, in_specs=placed, out_specs=P(("seq", "head"), None), check_vma=False
    )
```

profile of v0, /device:TPU:24, one launch (start us, length us, event | category | flops | bytes accessed | tf_op | source)
XLA Modules:
  0.0 847.9 jit_solution(1969970529256142345)
XLA Ops:
  6.5 3.9 convolution_convert_fusion
  37.0 2.8 convolution_multiply_fusion
  39.8 2.8 fusion.27
  42.6 158.7 %custom-call.3 = f32[4,8,1,64,64]{3,4,2,1,0:T(8,128)} custom-call(f32[4,8,1,64,64]{4,3,2,1,0:T(8,128)} %fusion.27), custom_call_target="InvertDiagBlocksLowerTriangular" | custom-call | tf_op jit(solution)/shard_map/triangular_solve | solution.py:95
  210.0 5.1 fusion.39
  215.2 5.5 multiply_subtract_fusion
  220.7 21.9 %while.39 = (s32[]{:T(128)}, f32[8,128,128]{2,1,0:T(8,128)}, f32[8,128,128]{2,1,0:T(8,128)S(1)}, f32[4,8,128,128]{3,2,1,0:T(8,128)}, f32[4,8,128,128]{3,2,1,0:T(8,128)}, /*index=5*/s32[]{:T(128)}, s32[]{:T(128)}) while((s32[]{:T(128)}, f32[8,128,128]{2,1,0:T(8,128)}, f32[8,128,128]{2,1,0:T(8,128)S(1)}, ...), condition=%wide.region_3.4_spmd.clone, body=%wide.region_2.3_spmd.clone.sunk | while | flops 402915328 | bytes 5768791 | solution.py:128
  221.8 2.6 convolution_add_fusion.11
  227.2 2.6 convolution_add_fusion.11
  232.7 2.6 convolution_add_fusion.11
  238.2 2.6 convolution_add_fusion.11
  242.6 537.2 %while.37 = (s32[]{:T(128)}, f32[8,128,128]{2,1,0:T(8,128)S(1)}, pred[]{:T(512)}, f32[8,128,128]{2,1,0:T(8,128)S(1)}, f32[8,128,128]{2,1,0:T(8,128)}, /*index=5*/f32[8,128,128]{2,1,0:T(8,128)}, s32[]{:T(128)}) while((s32[]{:T(128)}, f32[8,128,128]{2,1,0:T(8,128)S(1)}, pred[]{:T(512)}, f32[8,128,128]{2,1,0:T(8,128)S(1)}, ...), condition=%wide.region_5.6_spmd, body=%wide.region_4.5_spmd.sunk | while | flops 201588736 | bytes 7864466 | solution.py:138
  245.1 3.9 collective-permute-start
  249.0 8.9 %collective-permute-done = f32[8,128,128]{2,1,0:T(8,128)S(1)} collective-permute-done((f32[8,128,128]{2,1,0:T(8,128)}, f32[8,128,128]{2,1,0:T(8,128)S(1)}, u32[]{:S(2)}, u32[]{:S(2)}) %collective-permute-start) | collective-permute-done | bytes 524320 | tf_op jit(solution)/shard_map/while/body/eval_jaxpr/ppermute | solution.py:13
  264.4 10.9 %collective-permute-done = f32[8,128,128]{2,1,0:T(8,128)S(1)} collective-permute-done((f32[8,128,128]{2,1,0:T(8,128)}, f32[8,128,128]{2,1,0:T(8,128)S(1)}, u32[]{:S(2)}, u32[]{:S(2)}) %collective-permute-start) | collective-permute-done | bytes 524320 | tf_op jit(solution)/shard_map/while/body/eval_jaxpr/ppermute | solution.py:13
  281.7 10.9 %collective-permute-done = f32[8,128,128]{2,1,0:T(8,128)S(1)} collective-permute-done((f32[8,128,128]{2,1,0:T(8,128)}, f32[8,128,128]{2,1,0:T(8,128)S(1)}, u32[]{:S(2)}, u32[]{:S(2)}) %collective-permute-start) | collective-permute-done | bytes 524320 | tf_op jit(solution)/shard_map/while/body/eval_jaxpr/ppermute | solution.py:13
  299.0 10.9 %collective-permute-done = f32[8,128,128]{2,1,0:T(8,128)S(1)} collective-permute-done((f32[8,128,128]{2,1,0:T(8,128)}, f32[8,128,128]{2,1,0:T(8,128)S(1)}, u32[]{:S(2)}, u32[]{:S(2)}) %collective-permute-start) | collective-permute-done | bytes 524320 | tf_op jit(solution)/shard_map/while/body/eval_jaxpr/ppermute | solution.py:13
  316.4 10.9 %collective-permute-done = f32[8,128,128]{2,1,0:T(8,128)S(1)} collective-permute-done((f32[8,128,128]{2,1,0:T(8,128)}, f32[8,128,128]{2,1,0:T(8,128)S(1)}, u32[]{:S(2)}, u32[]{:S(2)}) %collective-permute-start) | collective-permute-done | bytes 524320 | tf_op jit(solution)/shard_map/while/body/eval_jaxpr/ppermute | solution.py:13
  333.7 10.9 %collective-permute-done = f32[8,128,128]{2,1,0:T(8,128)S(1)} collective-permute-done((f32[8,128,128]{2,1,0:T(8,128)}, f32[8,128,128]{2,1,0:T(8,128)S(1)}, u32[]{:S(2)}, u32[]{:S(2)}) %collective-permute-start) | collective-permute-done | bytes 524320 | tf_op jit(solution)/shard_map/while/body/eval_jaxpr/ppermute | solution.py:13
  351.0 10.9 %collective-permute-done = f32[8,128,128]{2,1,0:T(8,128)S(1)} collective-permute-done((f32[8,128,128]{2,1,0:T(8,128)}, f32[8,128,128]{2,1,0:T(8,128)S(1)}, u32[]{:S(2)}, u32[]{:S(2)}) %collective-permute-start) | collective-permute-done | bytes 524320 | tf_op jit(solution)/shard_map/while/body/eval_jaxpr/ppermute | solution.py:13
  368.4 10.9 %collective-permute-done = f32[8,128,128]{2,1,0:T(8,128)S(1)} collective-permute-done((f32[8,128,128]{2,1,0:T(8,128)}, f32[8,128,128]{2,1,0:T(8,128)S(1)}, u32[]{:S(2)}, u32[]{:S(2)}) %collective-permute-start) | collective-permute-done | bytes 524320 | tf_op jit(solution)/shard_map/while/body/eval_jaxpr/ppermute | solution.py:13
  385.7 10.9 %collective-permute-done = f32[8,128,128]{2,1,0:T(8,128)S(1)} collective-permute-done((f32[8,128,128]{2,1,0:T(8,128)}, f32[8,128,128]{2,1,0:T(8,128)S(1)}, u32[]{:S(2)}, u32[]{:S(2)}) %collective-permute-start) | collective-permute-done | bytes 524320 | tf_op jit(solution)/shard_map/while/body/eval_jaxpr/ppermute | solution.py:13
  403.0 10.9 %collective-permute-done = f32[8,128,128]{2,1,0:T(8,128)S(1)} collective-permute-done((f32[8,128,128]{2,1,0:T(8,128)}, f32[8,128,128]{2,1,0:T(8,128)S(1)}, u32[]{:S(2)}, u32[]{:S(2)}) %collective-permute-start) | collective-permute-done | bytes 524320 | tf_op jit(solution)/shard_map/while/body/eval_jaxpr/ppermute | solution.py:13
  420.4 10.9 %collective-permute-done = f32[8,128,128]{2,1,0:T(8,128)S(1)} collective-permute-done((f32[8,128,128]{2,1,0:T(8,128)}, f32[8,128,128]{2,1,0:T(8,128)S(1)}, u32[]{:S(2)}, u32[]{:S(2)}) %collective-permute-start) | collective-permute-done | bytes 524320 | tf_op jit(solution)/shard_map/while/body/eval_jaxpr/ppermute | solution.py:13
  437.7 10.9 %collective-permute-done = f32[8,128,128]{2,1,0:T(8,128)S(1)} collective-permute-done((f32[8,128,128]{2,1,0:T(8,128)}, f32[8,128,128]{2,1,0:T(8,128)S(1)}, u32[]{:S(2)}, u32[]{:S(2)}) %collective-permute-start) | collective-permute-done | bytes 524320 | tf_op jit(solution)/shard_map/while/body/eval_jaxpr/ppermute | solution.py:13
  455.0 10.9 %collective-permute-done = f32[8,128,128]{2,1,0:T(8,128)S(1)} collective-permute-done((f32[8,128,128]{2,1,0:T(8,128)}, f32[8,128,128]{2,1,0:T(8,128)S(1)}, u32[]{:S(2)}, u32[]{:S(2)}) %collective-permute-start) | collective-permute-done | bytes 524320 | tf_op jit(solution)/shard_map/while/body/eval_jaxpr/ppermute | solution.py:13
  472.3 10.9 %collective-permute-done = f32[8,128,128]{2,1,0:T(8,128)S(1)} collective-permute-done((f32[8,128,128]{2,1,0:T(8,128)}, f32[8,128,128]{2,1,0:T(8,128)S(1)}, u32[]{:S(2)}, u32[]{:S(2)}) %collective-permute-start) | collective-permute-done | bytes 524320 | tf_op jit(solution)/shard_map/while/body/eval_jaxpr/ppermute | solution.py:13
  489.7 10.9 %collective-permute-done = f32[8,128,128]{2,1,0:T(8,128)S(1)} collective-permute-done((f32[8,128,128]{2,1,0:T(8,128)}, f32[8,128,128]{2,1,0:T(8,128)S(1)}, u32[]{:S(2)}, u32[]{:S(2)}) %collective-permute-start) | collective-permute-done | bytes 524320 | tf_op jit(solution)/shard_map/while/body/eval_jaxpr/ppermute | solution.py:13
  507.0 10.9 %collective-permute-done = f32[8,128,128]{2,1,0:T(8,128)S(1)} collective-permute-done((f32[8,128,128]{2,1,0:T(8,128)}, f32[8,128,128]{2,1,0:T(8,128)S(1)}, u32[]{:S(2)}, u32[]{:S(2)}) %collective-permute-start) | collective-permute-done | bytes 524320 | tf_op jit(solution)/shard_map/while/body/eval_jaxpr/ppermute | solution.py:13
  524.3 10.9 %collective-permute-done = f32[8,128,128]{2,1,0:T(8,128)S(1)} collective-permute-done((f32[8,128,128]{2,1,0:T(8,128)}, f32[8,128,128]{2,1,0:T(8,128)S(1)}, u32[]{:S(2)}, u32[]{:S(2)}) %collective-permute-start) | collective-permute-done | bytes 524320 | tf_op jit(solution)/shard_map/while/body/eval_jaxpr/ppermute | solution.py:13
  541.7 10.9 %collective-permute-done = f32[8,128,128]{2,1,0:T(8,128)S(1)} collective-permute-done((f32[8,128,128]{2,1,0:T(8,128)}, f32[8,128,128]{2,1,0:T(8,128)S(1)}, u32[]{:S(2)}, u32[]{:S(2)}) %collective-permute-start) | collective-permute-done | bytes 524320 | tf_op jit(solution)/shard_map/while/body/eval_jaxpr/ppermute | solution.py:13
  559.0 10.9 %collective-permute-done = f32[8,128,128]{2,1,0:T(8,128)S(1)} collective-permute-done((f32[8,128,128]{2,1,0:T(8,128)}, f32[8,128,128]{2,1,0:T(8,128)S(1)}, u32[]{:S(2)}, u32[]{:S(2)}) %collective-permute-start) | collective-permute-done | bytes 524320 | tf_op jit(solution)/shard_map/while/body/eval_jaxpr/ppermute | solution.py:13
  576.3 10.9 %collective-permute-done = f32[8,128,128]{2,1,0:T(8,128)S(1)} collective-permute-done((f32[8,128,128]{2,1,0:T(8,128)}, f32[8,128,128]{2,1,0:T(8,128)S(1)}, u32[]{:S(2)}, u32[]{:S(2)}) %collective-permute-start) | collective-permute-done | bytes 524320 | tf_op jit(solution)/shard_map/while/body/eval_jaxpr/ppermute | solution.py:13
  593.7 10.9 %collective-permute-done = f32[8,128,128]{2,1,0:T(8,128)S(1)} collective-permute-done((f32[8,128,128]{2,1,0:T(8,128)}, f32[8,128,128]{2,1,0:T(8,128)S(1)}, u32[]{:S(2)}, u32[]{:S(2)}) %collective-permute-start) | collective-permute-done | bytes 524320 | tf_op jit(solution)/shard_map/while/body/eval_jaxpr/ppermute | solution.py:13
  611.0 10.9 %collective-permute-done = f32[8,128,128]{2,1,0:T(8,128)S(1)} collective-permute-done((f32[8,128,128]{2,1,0:T(8,128)}, f32[8,128,128]{2,1,0:T(8,128)S(1)}, u32[]{:S(2)}, u32[]{:S(2)}) %collective-permute-start) | collective-permute-done | bytes 524320 | tf_op jit(solution)/shard_map/while/body/eval_jaxpr/ppermute | solution.py:13
  628.3 10.9 %collective-permute-done = f32[8,128,128]{2,1,0:T(8,128)S(1)} collective-permute-done((f32[8,128,128]{2,1,0:T(8,128)}, f32[8,128,128]{2,1,0:T(8,128)S(1)}, u32[]{:S(2)}, u32[]{:S(2)}) %collective-permute-start) | collective-permute-done | bytes 524320 | tf_op jit(solution)/shard_map/while/body/eval_jaxpr/ppermute | solution.py:13
  645.6 10.9 %collective-permute-done = f32[8,128,128]{2,1,0:T(8,128)S(1)} collective-permute-done((f32[8,128,128]{2,1,0:T(8,128)}, f32[8,128,128]{2,1,0:T(8,128)S(1)}, u32[]{:S(2)}, u32[]{:S(2)}) %collective-permute-start) | collective-permute-done | bytes 524320 | tf_op jit(solution)/shard_map/while/body/eval_jaxpr/ppermute | solution.py:13
  663.0 10.9 %collective-permute-done = f32[8,128,128]{2,1,0:T(8,128)S(1)} collective-permute-done((f32[8,128,128]{2,1,0:T(8,128)}, f32[8,128,128]{2,1,0:T(8,128)S(1)}, u32[]{:S(2)}, u32[]{:S(2)}) %collective-permute-start) | collective-permute-done | bytes 524320 | tf_op jit(solution)/shard_map/while/body/eval_jaxpr/ppermute | solution.py:13
  680.3 10.9 %collective-permute-done = f32[8,128,128]{2,1,0:T(8,128)S(1)} collective-permute-done((f32[8,128,128]{2,1,0:T(8,128)}, f32[8,128,128]{2,1,0:T(8,128)S(1)}, u32[]{:S(2)}, u32[]{:S(2)}) %collective-permute-start) | collective-permute-done | bytes 524320 | tf_op jit(solution)/shard_map/while/body/eval_jaxpr/ppermute | solution.py:13
  697.6 10.9 %collective-permute-done = f32[8,128,128]{2,1,0:T(8,128)S(1)} collective-permute-done((f32[8,128,128]{2,1,0:T(8,128)}, f32[8,128,128]{2,1,0:T(8,128)S(1)}, u32[]{:S(2)}, u32[]{:S(2)}) %collective-permute-start) | collective-permute-done | bytes 524320 | tf_op jit(solution)/shard_map/while/body/eval_jaxpr/ppermute | solution.py:13
  715.0 10.9 %collective-permute-done = f32[8,128,128]{2,1,0:T(8,128)S(1)} collective-permute-done((f32[8,128,128]{2,1,0:T(8,128)}, f32[8,128,128]{2,1,0:T(8,128)S(1)}, u32[]{:S(2)}, u32[]{:S(2)}) %collective-permute-start) | collective-permute-done | bytes 524320 | tf_op jit(solution)/shard_map/while/body/eval_jaxpr/ppermute | solution.py:13
  732.3 10.9 %collective-permute-done = f32[8,128,128]{2,1,0:T(8,128)S(1)} collective-permute-done((f32[8,128,128]{2,1,0:T(8,128)}, f32[8,128,128]{2,1,0:T(8,128)S(1)}, u32[]{:S(2)}, u32[]{:S(2)}) %collective-permute-start) | collective-permute-done | bytes 524320 | tf_op jit(solution)/shard_map/while/body/eval_jaxpr/ppermute | solution.py:13
  749.6 10.9 %collective-permute-done = f32[8,128,128]{2,1,0:T(8,128)S(1)} collective-permute-done((f32[8,128,128]{2,1,0:T(8,128)}, f32[8,128,128]{2,1,0:T(8,128)S(1)}, u32[]{:S(2)}, u32[]{:S(2)}) %collective-permute-start) | collective-permute-done | bytes 524320 | tf_op jit(solution)/shard_map/while/body/eval_jaxpr/ppermute | solution.py:13
  767.0 10.9 %collective-permute-done = f32[8,128,128]{2,1,0:T(8,128)S(1)} collective-permute-done((f32[8,128,128]{2,1,0:T(8,128)}, f32[8,128,128]{2,1,0:T(8,128)S(1)}, u32[]{:S(2)}, u32[]{:S(2)}) %collective-permute-start) | collective-permute-done | bytes 524320 | tf_op jit(solution)/shard_map/while/body/eval_jaxpr/ppermute | solution.py:13
  779.8 17.0 %while.38 = (s32[]{:T(128)}, f32[8,128,128]{2,1,0:T(8,128)S(1)}, f32[4,8,64,128]{3,2,1,0:T(8,128)}, f32[4,8,128,128]{3,2,1,0:T(8,128)}, f32[4,8,128,128]{3,2,1,0...) while((s32[]{:T(128)}, f32[8,128,128]{2,1,0:T(8,128)S(1)}, ...), condition=%wide.region_8.9_spmd, body=%wide.region_7.8_spmd.sunk | while | flops 302186496 | bytes 4458581 | solution.py:139
  798.6 2.8 copy.48
  802.7 8.1 fusion.50
  810.9 28.4 %reduce-scatter.2.cloned.1.call-done = f32[64,2048]{1,0:T(8,128)} async-done(((f32[256,2048]{1,0:T(8,128)}), f32[64,2048]{1,0:T(8,128)}) %reduce-scatter.2.cloned.1.call-update) | async-done | bytes 524304 | tf_op jit(solution)/shard_map/reduce_scatter | solution.py:147
  (299 shorter events, 264.6 us)
Async XLA Ops:
  6.5 3.9 copy-start.9
  6.5 832.7 %reduce-scatter.2.cloned.1.call-start = ((), (), s32[]{:S(2)}) async-start(), calls=%async_computation.1 | async-start | bytes 2621440 | tf_op jit(solution)/shard_map/reduce_scatter | solution.py:147
  12.3 4.6 copy-start.23
  12.3 4.6 copy-start.25
  12.3 4.6 copy-start.26
  13.0 4.5 copy-start.32
  13.0 4.5 copy-start.10
  13.0 4.5 copy-start.17
  13.0 4.5 copy-start.28
  13.0 6.1 copy-start.18
  13.1 6.1 copy-start.29
  13.1 8.4 copy-start.30
  13.1 10.3 %copy-start.3 = (f32[8,128,128]{2,1,0:T(8,128)S(1)}, f32[8,128,128]{2,1,0:T(8,128)}, u32[]{:S(2)}) copy-start(f32[8,128,128]{2,1,0:T(8,128)} %param.37) | copy-start | bytes 1572868
  14.3 9.1 %collective-permute-start.1 = (bf16[3,2048]{1,0:T(4,128)(2,1)}, bf16[3,2048]{1,0:T(4,128)(2,1)}, u32[]{:S(2)}, u32[]{:S(2)}) collective-permute-start(bf16[3,2048]{1,0:T(4,128)(2,1)} %slice.63), channel_id=1, source_target_pairs={{0,4},{4,8},{8,12},{12,16},{16,20},{20,24},{24,28},{28,32},{32,36}... | collective-permute-start | bytes 36872 | tf_op jit(solution)/shard_map/ppermute | solution.py:13
  210.0 5.1 copy-start.21
  245.1 12.8 %collective-permute-start = (f32[8,128,128]{2,1,0:T(8,128)}, f32[8,128,128]{2,1,0:T(8,128)S(1)}, u32[]{:S(2)}, u32[]{:S(2)}) collective-permute-start(f32[8,128,128]{2,1,0:T(8,128)} %convolution_add_fusion.9), channel_id=1, source_target_pairs={{0,4},{4,8},{8,12},{12,16},{16,20},{20,24},{24,28},{28,32},{32,36}... | collective-permute-start | bytes 1572872 | tf_op jit(solution)/shard_map/while/body/eval_jaxpr/ppermute | solution.py:13
  262.5 12.8 %collective-permute-start = (f32[8,128,128]{2,1,0:T(8,128)}, f32[8,128,128]{2,1,0:T(8,128)S(1)}, u32[]{:S(2)}, u32[]{:S(2)}) collective-permute-start(f32[8,128,128]{2,1,0:T(8,128)} %convolution_add_fusion.9), channel_id=1, source_target_pairs={{0,4},{4,8},{8,12},{12,16},{16,20},{20,24},{24,28},{28,32},{32,36}... | collective-permute-start | bytes 1572872 | tf_op jit(solution)/shard_map/while/body/eval_jaxpr/ppermute | solution.py:13
  279.8 12.8 %collective-permute-start = (f32[8,128,128]{2,1,0:T(8,128)}, f32[8,128,128]{2,1,0:T(8,128)S(1)}, u32[]{:S(2)}, u32[]{:S(2)}) collective-permute-start(f32[8,128,128]{2,1,0:T(8,128)} %convolution_add_fusion.9), channel_id=1, source_target_pairs={{0,4},{4,8},{8,12},{12,16},{16,20},{20,24},{24,28},{28,32},{32,36}... | collective-permute-start | bytes 1572872 | tf_op jit(solution)/shard_map/while/body/eval_jaxpr/ppermute | solution.py:13
  297.1 12.8 %collective-permute-start = (f32[8,128,128]{2,1,0:T(8,128)}, f32[8,128,128]{2,1,0:T(8,128)S(1)}, u32[]{:S(2)}, u32[]{:S(2)}) collective-permute-start(f32[8,128,128]{2,1,0:T(8,128)} %convolution_add_fusion.9), channel_id=1, source_target_pairs={{0,4},{4,8},{8,12},{12,16},{16,20},{20,24},{24,28},{28,32},{32,36}... | collective-permute-start | bytes 1572872 | tf_op jit(solution)/shard_map/while/body/eval_jaxpr/ppermute | solution.py:13
  314.5 12.8 %collective-permute-start = (f32[8,128,128]{2,1,0:T(8,128)}, f32[8,128,128]{2,1,0:T(8,128)S(1)}, u32[]{:S(2)}, u32[]{:S(2)}) collective-permute-start(f32[8,128,128]{2,1,0:T(8,128)} %convolution_add_fusion.9), channel_id=1, source_target_pairs={{0,4},{4,8},{8,12},{12,16},{16,20},{20,24},{24,28},{28,32},{32,36}... | collective-permute-start | bytes 1572872 | tf_op jit(solution)/shard_map/while/body/eval_jaxpr/ppermute | solution.py:13
  331.8 12.8 %collective-permute-start = (f32[8,128,128]{2,1,0:T(8,128)}, f32[8,128,128]{2,1,0:T(8,128)S(1)}, u32[]{:S(2)}, u32[]{:S(2)}) collective-permute-start(f32[8,128,128]{2,1,0:T(8,128)} %convolution_add_fusion.9), channel_id=1, source_target_pairs={{0,4},{4,8},{8,12},{12,16},{16,20},{20,24},{24,28},{28,32},{32,36}... | collective-permute-start | bytes 1572872 | tf_op jit(solution)/shard_map/while/body/eval_jaxpr/ppermute | solution.py:13
  349.1 12.8 %collective-permute-start = (f32[8,128,128]{2,1,0:T(8,128)}, f32[8,128,128]{2,1,0:T(8,128)S(1)}, u32[]{:S(2)}, u32[]{:S(2)}) collective-permute-start(f32[8,128,128]{2,1,0:T(8,128)} %convolution_add_fusion.9), channel_id=1, source_target_pairs={{0,4},{4,8},{8,12},{12,16},{16,20},{20,24},{24,28},{28,32},{32,36}... | collective-permute-start | bytes 1572872 | tf_op jit(solution)/shard_map/while/body/eval_jaxpr/ppermute | solution.py:13
  366.4 12.8 %collective-permute-start = (f32[8,128,128]{2,1,0:T(8,128)}, f32[8,128,128]{2,1,0:T(8,128)S(1)}, u32[]{:S(2)}, u32[]{:S(2)}) collective-permute-start(f32[8,128,128]{2,1,0:T(8,128)} %convolution_add_fusion.9), channel_id=1, source_target_pairs={{0,4},{4,8},{8,12},{12,16},{16,20},{20,24},{24,28},{28,32},{32,36}... | collective-permute-start | bytes 1572872 | tf_op jit(solution)/shard_map/while/body/eval_jaxpr/ppermute | solution.py:13
  383.8 12.8 %collective-permute-start = (f32[8,128,128]{2,1,0:T(8,128)}, f32[8,128,128]{2,1,0:T(8,128)S(1)}, u32[]{:S(2)}, u32[]{:S(2)}) collective-permute-start(f32[8,128,128]{2,1,0:T(8,128)} %convolution_add_fusion.9), channel_id=1, source_target_pairs={{0,4},{4,8},{8,12},{12,16},{16,20},{20,24},{24,28},{28,32},{32,36}... | collective-permute-start | bytes 1572872 | tf_op jit(solution)/shard_map/while/body/eval_jaxpr/ppermute | solution.py:13
  401.1 12.8 %collective-permute-start = (f32[8,128,128]{2,1,0:T(8,128)}, f32[8,128,128]{2,1,0:T(8,128)S(1)}, u32[]{:S(2)}, u32[]{:S(2)}) collective-permute-start(f32[8,128,128]{2,1,0:T(8,128)} %convolution_add_fusion.9), channel_id=1, source_target_pairs={{0,4},{4,8},{8,12},{12,16},{16,20},{20,24},{24,28},{28,32},{32,36}... | collective-permute-start | bytes 1572872 | tf_op jit(solution)/shard_map/while/body/eval_jaxpr/ppermute | solution.py:13
  418.4 12.8 %collective-permute-start = (f32[8,128,128]{2,1,0:T(8,128)}, f32[8,128,128]{2,1,0:T(8,128)S(1)}, u32[]{:S(2)}, u32[]{:S(2)}) collective-permute-start(f32[8,128,128]{2,1,0:T(8,128)} %convolution_add_fusion.9), channel_id=1, source_target_pairs={{0,4},{4,8},{8,12},{12,16},{16,20},{20,24},{24,28},{28,32},{32,36}... | collective-permute-start | bytes 1572872 | tf_op jit(solution)/shard_map/while/body/eval_jaxpr/ppermute | solution.py:13
  435.8 12.8 %collective-permute-start = (f32[8,128,128]{2,1,0:T(8,128)}, f32[8,128,128]{2,1,0:T(8,128)S(1)}, u32[]{:S(2)}, u32[]{:S(2)}) collective-permute-start(f32[8,128,128]{2,1,0:T(8,128)} %convolution_add_fusion.9), channel_id=1, source_target_pairs={{0,4},{4,8},{8,12},{12,16},{16,20},{20,24},{24,28},{28,32},{32,36}... | collective-permute-start | bytes 1572872 | tf_op jit(solution)/shard_map/while/body/eval_jaxpr/ppermute | solution.py:13
  453.1 12.8 %collective-permute-start = (f32[8,128,128]{2,1,0:T(8,128)}, f32[8,128,128]{2,1,0:T(8,128)S(1)}, u32[]{:S(2)}, u32[]{:S(2)}) collective-permute-start(f32[8,128,128]{2,1,0:T(8,128)} %convolution_add_fusion.9), channel_id=1, source_target_pairs={{0,4},{4,8},{8,12},{12,16},{16,20},{20,24},{24,28},{28,32},{32,36}... | collective-permute-start | bytes 1572872 | tf_op jit(solution)/shard_map/while/body/eval_jaxpr/ppermute | solution.py:13
  470.4 12.8 %collective-permute-start = (f32[8,128,128]{2,1,0:T(8,128)}, f32[8,128,128]{2,1,0:T(8,128)S(1)}, u32[]{:S(2)}, u32[]{:S(2)}) collective-permute-start(f32[8,128,128]{2,1,0:T(8,128)} %convolution_add_fusion.9), channel_id=1, source_target_pairs={{0,4},{4,8},{8,12},{12,16},{16,20},{20,24},{24,28},{28,32},{32,36}... | collective-permute-start | bytes 1572872 | tf_op jit(solution)/shard_map/while/body/eval_jaxpr/ppermute | solution.py:13
  487.8 12.8 %collective-permute-start = (f32[8,128,128]{2,1,0:T(8,128)}, f32[8,128,128]{2,1,0:T(8,128)S(1)}, u32[]{:S(2)}, u32[]{:S(2)}) collective-permute-start(f32[8,128,128]{2,1,0:T(8,128)} %convolution_add_fusion.9), channel_id=1, source_target_pairs={{0,4},{4,8},{8,12},{12,16},{16,20},{20,24},{24,28},{28,32},{32,36}... | collective-permute-start | bytes 1572872 | tf_op jit(solution)/shard_map/while/body/eval_jaxpr/ppermute | solution.py:13
  505.1 12.8 %collective-permute-start = (f32[8,128,128]{2,1,0:T(8,128)}, f32[8,128,128]{2,1,0:T(8,128)S(1)}, u32[]{:S(2)}, u32[]{:S(2)}) collective-permute-start(f32[8,128,128]{2,1,0:T(8,128)} %convolution_add_fusion.9), channel_id=1, source_target_pairs={{0,4},{4,8},{8,12},{12,16},{16,20},{20,24},{24,28},{28,32},{32,36}... | collective-permute-start | bytes 1572872 | tf_op jit(solution)/shard_map/while/body/eval_jaxpr/ppermute | solution.py:13
  522.4 12.8 %collective-permute-start = (f32[8,128,128]{2,1,0:T(8,128)}, f32[8,128,128]{2,1,0:T(8,128)S(1)}, u32[]{:S(2)}, u32[]{:S(2)}) collective-permute-start(f32[8,128,128]{2,1,0:T(8,128)} %convolution_add_fusion.9), channel_id=1, source_target_pairs={{0,4},{4,8},{8,12},{12,16},{16,20},{20,24},{24,28},{28,32},{32,36}... | collective-permute-start | bytes 1572872 | tf_op jit(solution)/shard_map/while/body/eval_jaxpr/ppermute | solution.py:13
  539.8 12.8 %collective-permute-start = (f32[8,128,128]{2,1,0:T(8,128)}, f32[8,128,128]{2,1,0:T(8,128)S(1)}, u32[]{:S(2)}, u32[]{:S(2)}) collective-permute-start(f32[8,128,128]{2,1,0:T(8,128)} %convolution_add_fusion.9), channel_id=1, source_target_pairs={{0,4},{4,8},{8,12},{12,16},{16,20},{20,24},{24,28},{28,32},{32,36}... | collective-permute-start | bytes 1572872 | tf_op jit(solution)/shard_map/while/body/eval_jaxpr/ppermute | solution.py:13
  557.1 12.8 %collective-permute-start = (f32[8,128,128]{2,1,0:T(8,128)}, f32[8,128,128]{2,1,0:T(8,128)S(1)}, u32[]{:S(2)}, u32[]{:S(2)}) collective-permute-start(f32[8,128,128]{2,1,0:T(8,128)} %convolution_add_fusion.9), channel_id=1, source_target_pairs={{0,4},{4,8},{8,12},{12,16},{16,20},{20,24},{24,28},{28,32},{32,36}... | collective-permute-start | bytes 1572872 | tf_op jit(solution)/shard_map/while/body/eval_jaxpr/ppermute | solution.py:13
  574.4 12.8 %collective-permute-start = (f32[8,128,128]{2,1,0:T(8,128)}, f32[8,128,128]{2,1,0:T(8,128)S(1)}, u32[]{:S(2)}, u32[]{:S(2)}) collective-permute-start(f32[8,128,128]{2,1,0:T(8,128)} %convolution_add_fusion.9), channel_id=1, source_target_pairs={{0,4},{4,8},{8,12},{12,16},{16,20},{20,24},{24,28},{28,32},{32,36}... | collective-permute-start | bytes 1572872 | tf_op jit(solution)/shard_map/while/body/eval_jaxpr/ppermute | solution.py:13
  591.7 12.8 %collective-permute-start = (f32[8,128,128]{2,1,0:T(8,128)}, f32[8,128,128]{2,1,0:T(8,128)S(1)}, u32[]{:S(2)}, u32[]{:S(2)}) collective-permute-start(f32[8,128,128]{2,1,0:T(8,128)} %convolution_add_fusion.9), channel_id=1, source_target_pairs={{0,4},{4,8},{8,12},{12,16},{16,20},{20,24},{24,28},{28,32},{32,36}... | collective-permute-start | bytes 1572872 | tf_op jit(solution)/shard_map/while/body/eval_jaxpr/ppermute | solution.py:13
  609.1 12.8 %collective-permute-start = (f32[8,128,128]{2,1,0:T(8,128)}, f32[8,128,128]{2,1,0:T(8,128)S(1)}, u32[]{:S(2)}, u32[]{:S(2)}) collective-permute-start(f32[8,128,128]{2,1,0:T(8,128)} %convolution_add_fusion.9), channel_id=1, source_target_pairs={{0,4},{4,8},{8,12},{12,16},{16,20},{20,24},{24,28},{28,32},{32,36}... | collective-permute-start | bytes 1572872 | tf_op jit(solution)/shard_map/while/body/eval_jaxpr/ppermute | solution.py:13
  626.4 12.8 %collective-permute-start = (f32[8,128,128]{2,1,0:T(8,128)}, f32[8,128,128]{2,1,0:T(8,128)S(1)}, u32[]{:S(2)}, u32[]{:S(2)}) collective-permute-start(f32[8,128,128]{2,1,0:T(8,128)} %convolution_add_fusion.9), channel_id=1, source_target_pairs={{0,4},{4,8},{8,12},{12,16},{16,20},{20,24},{24,28},{28,32},{32,36}... | collective-permute-start | bytes 1572872 | tf_op jit(solution)/shard_map/while/body/eval_jaxpr/ppermute | solution.py:13
  643.7 12.8 %collective-permute-start = (f32[8,128,128]{2,1,0:T(8,128)}, f32[8,128,128]{2,1,0:T(8,128)S(1)}, u32[]{:S(2)}, u32[]{:S(2)}) collective-permute-start(f32[8,128,128]{2,1,0:T(8,128)} %convolution_add_fusion.9), channel_id=1, source_target_pairs={{0,4},{4,8},{8,12},{12,16},{16,20},{20,24},{24,28},{28,32},{32,36}... | collective-permute-start | bytes 1572872 | tf_op jit(solution)/shard_map/while/body/eval_jaxpr/ppermute | solution.py:13
  661.1 12.8 %collective-permute-start = (f32[8,128,128]{2,1,0:T(8,128)}, f32[8,128,128]{2,1,0:T(8,128)S(1)}, u32[]{:S(2)}, u32[]{:S(2)}) collective-permute-start(f32[8,128,128]{2,1,0:T(8,128)} %convolution_add_fusion.9), channel_id=1, source_target_pairs={{0,4},{4,8},{8,12},{12,16},{16,20},{20,24},{24,28},{28,32},{32,36}... | collective-permute-start | bytes 1572872 | tf_op jit(solution)/shard_map/while/body/eval_jaxpr/ppermute | solution.py:13
  678.4 12.8 %collective-permute-start = (f32[8,128,128]{2,1,0:T(8,128)}, f32[8,128,128]{2,1,0:T(8,128)S(1)}, u32[]{:S(2)}, u32[]{:S(2)}) collective-permute-start(f32[8,128,128]{2,1,0:T(8,128)} %convolution_add_fusion.9), channel_id=1, source_target_pairs={{0,4},{4,8},{8,12},{12,16},{16,20},{20,24},{24,28},{28,32},{32,36}... | collective-permute-start | bytes 1572872 | tf_op jit(solution)/shard_map/while/body/eval_jaxpr/ppermute | solution.py:13
  695.7 12.8 %collective-permute-start = (f32[8,128,128]{2,1,0:T(8,128)}, f32[8,128,128]{2,1,0:T(8,128)S(1)}, u32[]{:S(2)}, u32[]{:S(2)}) collective-permute-start(f32[8,128,128]{2,1,0:T(8,128)} %convolution_add_fusion.9), channel_id=1, source_target_pairs={{0,4},{4,8},{8,12},{12,16},{16,20},{20,24},{24,28},{28,32},{32,36}... | collective-permute-start | bytes 1572872 | tf_op jit(solution)/shard_map/while/body/eval_jaxpr/ppermute | solution.py:13
  713.1 12.8 %collective-permute-start = (f32[8,128,128]{2,1,0:T(8,128)}, f32[8,128,128]{2,1,0:T(8,128)S(1)}, u32[]{:S(2)}, u32[]{:S(2)}) collective-permute-start(f32[8,128,128]{2,1,0:T(8,128)} %convolution_add_fusion.9), channel_id=1, source_target_pairs={{0,4},{4,8},{8,12},{12,16},{16,20},{20,24},{24,28},{28,32},{32,36}... | collective-permute-start | bytes 1572872 | tf_op jit(solution)/shard_map/while/body/eval_jaxpr/ppermute | solution.py:13
  730.4 12.8 %collective-permute-start = (f32[8,128,128]{2,1,0:T(8,128)}, f32[8,128,128]{2,1,0:T(8,128)S(1)}, u32[]{:S(2)}, u32[]{:S(2)}) collective-permute-start(f32[8,128,128]{2,1,0:T(8,128)} %convolution_add_fusion.9), channel_id=1, source_target_pairs={{0,4},{4,8},{8,12},{12,16},{16,20},{20,24},{24,28},{28,32},{32,36}... | collective-permute-start | bytes 1572872 | tf_op jit(solution)/shard_map/while/body/eval_jaxpr/ppermute | solution.py:13
  747.7 12.8 %collective-permute-start = (f32[8,128,128]{2,1,0:T(8,128)}, f32[8,128,128]{2,1,0:T(8,128)S(1)}, u32[]{:S(2)}, u32[]{:S(2)}) collective-permute-start(f32[8,128,128]{2,1,0:T(8,128)} %convolution_add_fusion.9), channel_id=1, source_target_pairs={{0,4},{4,8},{8,12},{12,16},{16,20},{20,24},{24,28},{28,32},{32,36}... | collective-permute-start | bytes 1572872 | tf_op jit(solution)/shard_map/while/body/eval_jaxpr/ppermute | solution.py:13
  765.0 12.8 %collective-permute-start = (f32[8,128,128]{2,1,0:T(8,128)}, f32[8,128,128]{2,1,0:T(8,128)S(1)}, u32[]{:S(2)}, u32[]{:S(2)}) collective-permute-start(f32[8,128,128]{2,1,0:T(8,128)} %convolution_add_fusion.9), channel_id=1, source_target_pairs={{0,4},{4,8},{8,12},{12,16},{16,20},{20,24},{24,28},{28,32},{32,36}... | collective-permute-start | bytes 1572872 | tf_op jit(solution)/shard_map/while/body/eval_jaxpr/ppermute | solution.py:13
  796.8 5.9 copy-start.11
  796.8 5.9 copy-start.27
  (48 other events, 68.7 us)
Sparse Core Ops, SparseCore 0:
  811.0 28.2 reduce-scatter.1
where the time goes:
time: 854 us; the launch traced here: 848 us
  waiting for transfers between devices  364 us (43%)
  other arithmetic  207 us (24%)
  matrix products  151 us (18%)
  starting transfers between devices  63.1 us (7%)
  local copies, waits for them, and re-layouts  47.8 us (6%)
  between operations  13.9 us (2%)
    ppermute x32, waiting for transfers between devices, passed_along(): return lax.ppermute(block, axis, route)  336 us
    another operation x4, other arithmetic, on_device(): lax.linalg.triangular_solve(system, rhs, left_side=True, lower=True, unit...  160 us
    dot_general x31, matrix products, relay(): jnp.einsum('hde,hev->hdv', local_map, incoming, precision=peak_magnitude)  79 us
    ppermute x32, starting transfers between devices, passed_along(): return lax.ppermute(block, axis, route)  63.1 us
    select_n x31, other arithmetic, relay(): return jnp.where(position == 0, state_in, arrived)  34.1 us
    while x74, local copies, waits for them, and re-layouts  31 us
    reduce_scatter x1, waiting for transfers between devices, on_device(): lax.psum_scatter(jnp.dot(normed, w_out, preferred_element_type=jnp.float3...  28.4 us
    dot_general x8, matrix products, advance(): jnp.einsum('hde,hev->hdv', trans, running_state, precision=peak_magnitude)  18 us
  transfers between devices with their start and end apart: 33, of which 32 were waited for; matrix products, arithmetic and copies ran while one was open for 1% of the time, Pallas kernels for 0%

commit v1 on v0

v1 whole, which is shorter than its diff:
```python
import jax
import jax.numpy as jnp
from jax import lax
from jax.experimental import pallas as pl
from jax.experimental.pallas import tpu as pltpu
from jax.sharding import PartitionSpec as P

MESH = pl.DeviceIdType.MESH
F32 = jnp.float32
BF16 = jnp.bfloat16
HALO = 16
OWN = 256
ROWS = 512
DM = 2048
CH = 128
NC = ROWS // CH
HEADS = 4
CHIPS = 16
MSG = 208


def dot(a, b):
    return jnp.dot(a, b, preferred_element_type=F32)


def dot_nt(a, b):
    return lax.dot_general(a, b, (((1,), (1,)), ((), ())), preferred_element_type=F32)


def silu(u):
    return u * jax.nn.sigmoid(u)


def kernel(
    hidden, w_query, w_key, w_value, w_gate_z, w_decay, w_beta, conv_query, conv_key, conv_value,
    decay_log, decay_bias, beta_bias, norm_gain, w_out, state_in,
    out,
    hid, wbuf, wdec, wbet, wo, st0, raw, qs, ks, vs, zs, cum, cumt, beta, low, tri, att, uw, ee, sb, ab,
    reach, outloc, send, recv, step_out, entering, nsend, nfull, rs_send, rs_relay, rs_arr, rs_own, rs_hold,
    lsem, wsem, xsem, hsem, msend, mrecv, osend, orecv, nsem, rsend, rrecv,
):
    seq = lax.axis_index("seq")
    xx = lax.axis_index("head")
    chip = seq // 2
    core = seq % 2
    other = 1 - core
    partner = (chip * 2 + other, xx)
    nxt = lax.rem(chip + 1, CHIPS)
    prv = lax.rem(chip + CHIPS - 1, CHIPS)
    right = lax.rem(xx + 1, 4)
    left = lax.rem(xx + 3, 4)
    across = lax.rem(xx + 2, 4)

    def at_x(x):
        return (seq, x)

    def local(src, dst, sem):
        return pltpu.make_async_copy(src, dst, sem)

    def remote(src, dst, s_sem, r_sem, device):
        return pltpu.make_async_remote_copy(
            src_ref=src, dst_ref=dst, send_sem=s_sem, recv_sem=r_sem, device_id=device, device_id_type=MESH
        )

    mine = pl.ds(pl.multiple_of(HALO + core * OWN, 16), OWN)
    theirs = pl.ds(pl.multiple_of(HALO + other * OWN, 16), OWN)
    col256 = pl.ds(pl.multiple_of(core * 256, 256), 256)

    own_copy = local(hidden, hid.at[mine, :], lsem.at[0])
    own_copy.start()
    w_copies = [
        local(w_query.at[:, col256], wbuf.at[0], wsem.at[0]),
        local(w_key.at[:, col256], wbuf.at[1], wsem.at[1]),
    ]
    for i in range(2):
        cols = pl.ds(pl.multiple_of(core * 512 + i * 256, 256), 256)
        w_copies.append(local(w_value.at[:, cols], wbuf.at[2 + i], wsem.at[2 + i]))
    for i in range(2):
        cols = pl.ds(pl.multiple_of(core * 512 + i * 256, 256), 256)
        w_copies.append(local(w_gate_z.at[:, cols], wbuf.at[4 + i], wsem.at[4 + i]))
    dec_copy = local(w_decay, wdec, lsem.at[1])
    bet_copy = local(w_beta, wbet, lsem.at[2])
    for cp in w_copies[:2]:
        cp.start()
    dec_copy.start()
    bet_copy.start()
    for cp in w_copies[2:]:
        cp.start()
    owner_head = core * HEADS + chip // 4
    owner_slot = chip // 2
    st_copy = local(state_in.at[owner_head], st0, lsem.at[3])
    st_copy.start()
    wo_copy = local(w_out, wo, lsem.at[4])
    wo_copy.start()

    barrier = pltpu.get_barrier_semaphore()

    def greet(device):
        pl.semaphore_signal(barrier, inc=1, device_id=device, device_id_type=MESH)

    greet(partner)
    greet((lax.select(core == 1, nxt * 2, prv * 2 + 1), xx))
    greet(at_x(right))
    greet(at_x(left))

    def greet_chip(k, carry):
        greet((lax.rem(chip + k, CHIPS) * 2 + core, xx))
        return carry

    lax.fori_loop(1, CHIPS, greet_chip, 0)
    pl.semaphore_wait(barrier, 19)

    swap = remote(hidden, hid.at[mine, :], xsem.at[0], xsem.at[1], partner)
    swap.start()
    tail = hidden.at[pl.ds(OWN - HALO, HALO), :]
    halo0 = remote(tail, hid.at[pl.ds(0, HALO), :], hsem.at[0], hsem.at[2], (nxt * 2, xx))
    halo1 = remote(tail, hid.at[pl.ds(0, HALO), :], hsem.at[1], hsem.at[2], (nxt * 2 + 1, xx))

    @pl.when(core == 1)
    def _():
        halo0.start()
        halo1.start()

    own_copy.wait()
    swap.wait_recv()
    halo0.wait_recv()

    @pl.when(chip == 0)
    def _():
        hid[pl.ds(0, HALO), :] = jnp.zeros((HALO, DM), BF16)

    taps_of = (
        lambda: conv_query[:, col256].astype(F32),
        lambda: conv_key[:, col256].astype(F32),
        lambda: conv_value[:, pl.ds(pl.multiple_of(core * 512, 256), 256)].astype(F32),
        lambda: conv_value[:, pl.ds(pl.multiple_of(core * 512 + 256, 256), 256)].astype(F32),
    )
    for b in range(4):
        w_copies[b].wait()

        def rows_of(t, carry, b=b):
            r = pl.ds(pl.multiple_of(t * 176, 16), 176)
            raw[b, r, :] = dot(hid[r, :], wbuf[b]).astype(BF16).astype(F32)
            return carry

        lax.fori_loop(0, 3, rows_of, 0)
        taps = taps_of[b]()
        for t in range(NC):
            pre = jnp.zeros((CH, 256), F32)
            for i in range(4):
                pre = pre + taps[i : i + 1, :] * raw[b, pl.ds(HALO - 3 + i + t * CH, CH), :]
            act = silu(pre)
            r = pl.ds(t * CH, CH)
            if b < 2:
                for g in range(2):
                    a = act[:, g * 128 : (g + 1) * 128]
                    n = a * lax.rsqrt(jnp.sum(a * a, axis=-1, keepdims=True) + 1e-6)
                    if b == 0:
                        qs[r, g * 128 : (g + 1) * 128] = (n * 128 ** (-0.5)).astype(BF16)
                    else:
                        ks[r, g * 128 : (g + 1) * 128] = n.astype(BF16)
            else:
                vs[r, (b - 2) * 256 : (b - 1) * 256] = act

    dec_copy.wait()
    bet_copy.wait()
    lane = lax.broadcasted_iota(jnp.int32, (1, HEADS), 1)

    def lanes_of(ref):
        v = jnp.zeros((1, HEADS), F32)
        for h in range(HEADS):
            v = jnp.where(lane == h, ref[core * HEADS + h], v)
        return v

    rate = -jnp.exp(lanes_of(decay_log))
    d_bias = lanes_of(decay_bias)
    b_bias = lanes_of(beta_bias)
    ti = lax.broadcasted_iota(jnp.int32, (CH, CH), 0)
    tj = lax.broadcasted_iota(jnp.int32, (CH, CH), 1)
    incl = ti >= tj
    ones_low = jnp.where(incl, 1.0, 0.0).astype(F32)
    for t in range(NC):
        hrows = hid[pl.ds(HALO + t * CH, CH), :]
        gd = dot(hrows, wdec[...])
        gb = dot(hrows, wbet[...])
        gd = jnp.where(core == 0, gd[:, :HEADS], gd[:, HEADS:])
        gb = jnp.where(core == 0, gb[:, :HEADS], gb[:, HEADS:])
        u = gd + d_bias
        soft = jnp.maximum(u, 0.0) + jnp.log1p(jnp.exp(-jnp.abs(u)))
        glog = jnp.concatenate([rate * soft, jnp.zeros((CH, 128 - HEADS), F32)], 1)
        cm = jnp.dot(ones_low, glog, precision=lax.Precision.HIGHEST, preferred_element_type=F32)
        cum[t] = cm
        cumt[t] = cm.T[:8, :]
        beta[t] = jnp.concatenate([jax.nn.sigmoid(gb + b_bias), jnp.zeros((CH, 128 - HEADS), F32)], 1)

    def systems(c, carry):
        r = pl.ds(pl.multiple_of(c * CH, CH), CH)
        cc_all = cum[c]
        cr_all = cumt[c]
        be_all = beta[c]
        for g in range(2):
            k = ks[r, g * 128 : (g + 1) * 128]
            q = qs[r, g * 128 : (g + 1) * 128]
            both = dot_nt(jnp.concatenate([k, q], 0), k)
            kk, qk = both[:CH], both[CH:]
            for e in range(2):
                h = 2 * g + e
                diff = cc_all[:, h : h + 1] - cr_all[h : h + 1, :]
                ratio = jnp.exp(jnp.where(incl, diff, -1e30))
                lo = jnp.where(ti > tj, be_all[:, h : h + 1] * ratio * kk, 0.0)
                low[c * 2 + g, :, e * 128 : (e + 1) * 128] = lo.astype(BF16)
                att[c * 4 + h] = (ratio * qk).astype(BF16)
                tri[c * 2 + g, :, e * 128 : (e + 1) * 128] = jnp.where(
                    ti == tj, 1.0, jnp.where((ti ^ tj) == 1, -lo, 0.0)
                ).astype(BF16)
        return carry

    lax.fori_loop(0, NC, systems, 0)

    z128 = jnp.zeros((CH, CH), BF16)

    def pair_diag(m):
        return jnp.concatenate(
            [jnp.concatenate([m[:, :128], z128], 1), jnp.concatenate([z128, m[:, 128:]], 1)], 0
        )

    pi = lax.broadcasted_iota(jnp.int32, (CH, 256), 0)
    pj = lax.broadcasted_iota(jnp.int32, (CH, 256), 1) % 128
    pxor = pi ^ pj

    def double(level, size):
        mask = (pxor >= size) & (pxor < 2 * size)
        prods = []
        for p in range(8):
            lm = jnp.where(mask, low[p].astype(F32), 0.0).astype(BF16)
            prods.append(dot(tri[p], pair_diag(lm)).astype(BF16))
        for p in range(8):
            t_old = tri[p]
            y = dot(prods[p], pair_diag(t_old))
            tri[p] = (t_old.astype(F32) - y).astype(BF16)
        return size * 2

    lax.fori_loop(0, 6, double, jnp.int32(2))

    def unit(c, carry):
        r = pl.ds(pl.multiple_of(c * CH, CH), CH)
        cc_all = cum[c]
        cr_all = cumt[c]
        be_all = beta[c]
        for g in range(2):
            k = ks[r, g * 128 : (g + 1) * 128].astype(F32)
            kt = k.T
            for e in range(2):
                h = 2 * g + e
                be = be_all[:, h : h + 1]
                cc = cc_all[:, h : h + 1]
                cr = cr_all[h : h + 1, :]
                tail_w = jnp.exp(cr[:, 127:128] - cr)
                rhs = jnp.concatenate([be * vs[r, h * 128 : (h + 1) * 128], (be * jnp.exp(cc)) * k], 1)
                u = dot(tri[c * 2 + g, :, e * 128 : (e + 1) * 128], rhs.astype(BF16)).astype(BF16)
                uw[c * 4 + h] = u
                ee[c * 4 + h] = dot((kt * tail_w).astype(BF16), u)
        return carry

    lax.fori_loop(0, NC, unit, 0)

    row16 = lax.broadcasted_iota(jnp.int32, (16, 128), 0)
    s_cur, b_cur, a_cur = [], [], []
    for h in range(HEADS):
        e0 = ee[h]
        s_cur.append(e0[:, :128])
        b_cur.append(-e0[:, 128:])
        a_cur.append(jnp.exp(cumt[0, h : h + 1, 127:128]))
        sb[h] = jnp.zeros((128, 256), BF16)
        ab[0, h : h + 1, :] = jnp.ones((1, 128), F32)
    for c in range(1, NC):
        for h in range(HEADS):
            s, bm, a = s_cur[h], b_cur[h], a_cur[h]
            packed = jnp.concatenate([s, bm], 1).astype(BF16)
            sb[c * 4 + h] = packed
            ab[c, h : h + 1, :] = jnp.broadcast_to(a, (1, 128))
            e_c = ee[c * 4 + h]
            m_c = e_c[:, 128:]
            p = dot(m_c.astype(BF16), packed)
            al = jnp.exp(cumt[c, h : h + 1, 127:128])
            s_cur[h] = al * s - p[:, :128] + e_c[:, :128]
            b_cur[h] = al * bm - a * m_c - p[:, 128:]
            a_cur[h] = a * al
    for h in range(HEADS):
        bt = b_cur[h].T.astype(BF16)
        s_t = s_cur[h].T.astype(BF16)
        a_full = jnp.broadcast_to(a_cur[h], (16, 128))
        a_hi = a_full.astype(BF16).astype(F32)
        a_rows = jnp.where(row16 < 8, a_hi, a_full - a_hi).astype(BF16)
        for half in range(2):
            o = 2 * h + half
            send[o, 0:128, :] = bt
            send[o, 128:192, :] = s_t[half * 64 : (half + 1) * 64, :]
            send[o, 192:208, :] = a_rows

    def to_owner(o):
        return remote(send.at[o], recv.at[chip], msend.at[o], mrecv.at[chip], ((2 * o + core) * 2 + core, xx))

    for o in range(8):
        @pl.when(2 * o + core != chip)
        def _(o=o):
            to_owner(o).start()

        @pl.when(2 * o + core == chip)
        def _(o=o):
            recv[chip] = send[o]

    def local_part(c, carry):
        r = pl.ds(pl.multiple_of(c * CH, CH), CH)
        cc_all = cum[c]
        a_all = ab[c]
        for h in range(HEADS):
            g = h // 2
            q = qs[r, g * 128 : (g + 1) * 128].astype(F32)
            o = dot(att[c * 4 + h], uw[c * 4 + h])
            qeff = jnp.exp(cc_all[:, h : h + 1]) * q - o[:, 128:]
            rr = dot(qeff.astype(BF16), sb[c * 4 + h])
            outloc[r, h * 128 : (h + 1) * 128] = o[:, :128] + rr[:, :128]
            reach[r, h * 128 : (h + 1) * 128] = (a_all[h : h + 1, :] * qeff + rr[:, 128:]).astype(BF16)
        return carry

    lax.fori_loop(0, NC, local_part, 0)

    owns = lax.rem(chip, 2) == core
    st_copy.wait()

    def give(i):
        return remote(step_out.at[i], entering.at[owner_slot], osend.at[i], orecv.at[owner_slot], (i * 2 + core, xx))

    @pl.when(owns)
    def _():
        for i in range(CHIPS):
            @pl.when(i != chip)
            def _(i=i):
                remote(send.at[0], recv.at[i], msend.at[0], mrecv.at[i], partner).wait_recv()
        st_t = st0[...].T
        s = jnp.where(lax.rem(owner_slot, 2) == 0, st_t[:64], st_t[64:])
        for i in range(CHIPS):
            sbf = s.astype(BF16)
            step_out[i] = sbf

            @pl.when(i != chip)
            def _(i=i):
                give(i).start()

            if i < CHIPS - 1:
                a = recv[i, 192:208, :].astype(F32)
                s = (a[0:1, :] + a[8:9, :]) * s + dot(sbf, recv[i, 0:128, :]) + recv[i, 128:192, :].astype(F32)
        entering[owner_slot] = step_out[chip]

    for b in range(2):
        w_copies[4 + b].wait()
    gain = jnp.concatenate([norm_gain[...].reshape(1, 128)] * 2, 1)

    def gate_rows(t, carry):
        r = pl.ds(pl.multiple_of(t * CH, CH), CH)
        h_rows = hid[pl.ds(pl.multiple_of(HALO + t * CH, 16), CH), :]
        for b in range(2):
            zs[r, b * 256 : (b + 1) * 256] = silu(dot(h_rows, wbuf[4 + b])) * gain
        return carry

    lax.fori_loop(0, NC, gate_rows, 0)

    for o in range(8):
        @pl.when(2 * o + core != chip)
        def _(o=o):
            remote(step_out.at[0], entering.at[o], osend.at[0], orecv.at[o], partner).wait_recv()

    def finish(base, put):
        for t in range(2):
            r = pl.ds(pl.multiple_of(base + t * CH, CH), CH)
            for h in range(HEADS):
                cols = slice(h * 128, (h + 1) * 128)
                s_t = jnp.concatenate([entering[2 * h], entering[2 * h + 1]], 0)
                o = outloc[r, cols] + dot_nt(reach[r, cols], s_t)
                n = o * lax.rsqrt(jnp.mean(o * o, axis=-1, keepdims=True) + 1e-6) * zs[r, cols]
                put(t, cols, n.astype(BF16))

    def put_send(t, cols, v):
        nsend[t * CH : (t + 1) * CH, cols] = v

    def put_own(t, cols, v):
        nfull[core, t * CH : (t + 1) * CH, cols] = v

    finish(other * OWN, put_send)
    n_swap = remote(nsend, nfull.at[core], nsem.at[0], nsem.at[1], partner)
    n_swap.start()
    finish(core * OWN, put_own)
    wo_copy.wait()
    n_swap.wait_recv()

    def block(x, n0, width):
        r = pl.ds(pl.multiple_of(x * 64, 64), 64)
        cols = slice(n0, n0 + width)
        return dot(nfull[0, r, :], wo[0:512, cols]) + dot(nfull[1, r, :], wo[512:1024, cols])

    def fill(dst, x, n0):
        for j in range(2):
            dst[:, j * 512 : (j + 1) * 512] = block(x, n0 + j * 512, 512).astype(BF16)

    relay_r = remote(rs_send.at[0], rs_relay.at[0], rsend.at[0], rrecv.at[0], at_x(right))
    relay_l = remote(rs_send.at[1], rs_relay.at[1], rsend.at[1], rrecv.at[1], at_x(left))
    direct_r = remote(rs_send.at[2], rs_arr.at[0], rsend.at[2], rrecv.at[2], at_x(right))
    direct_l = remote(rs_send.at[3], rs_arr.at[1], rsend.at[3], rrecv.at[3], at_x(left))
    sum_r = remote(rs_send.at[4], rs_arr.at[2], rsend.at[4], rrecv.at[4], at_x(right))
    sum_l = remote(rs_send.at[5], rs_arr.at[3], rsend.at[5], rrecv.at[5], at_x(left))
    fill(rs_send.at[0], across, 0)
    relay_r.start()
    fill(rs_send.at[1], across, 1024)
    relay_l.start()
    fill(rs_send.at[2], right, 1024)
    direct_r.start()
    fill(rs_send.at[3], left, 0)
    direct_l.start()
    for j in range(2):
        rs_hold[0, :, j * 512 : (j + 1) * 512] = block(right, j * 512, 512)
    for j in range(2):
        rs_hold[1, :, j * 512 : (j + 1) * 512] = block(left, 1024 + j * 512, 512)
    relay_r.wait_recv()
    rs_send[4] = (rs_hold[0] + rs_relay[0].astype(F32)).astype(BF16)
    sum_r.start()
    relay_l.wait_recv()
    rs_send[5] = (rs_hold[1] + rs_relay[1].astype(F32)).astype(BF16)
    sum_l.start()
    for j in range(4):
        rs_own[:, j * 512 : (j + 1) * 512] = block(xx, j * 512, 512)
    direct_r.wait_recv()
    direct_l.wait_recv()
    sum_r.wait_recv()
    sum_l.wait_recv()
    out[:, 0:1024] = (rs_own[:, 0:1024] + rs_arr[1].astype(F32) + rs_arr[2].astype(F32)).astype(BF16)
    out[:, 1024:2048] = (rs_own[:, 1024:2048] + rs_arr[0].astype(F32) + rs_arr[3].astype(F32)).astype(BF16)

    swap.wait_send()

    @pl.when(core == 1)
    def _():
        halo0.wait_send()
        halo1.wait_send()

    for o in range(8):
        @pl.when(2 * o + core != chip)
        def _(o=o):
            to_owner(o).wait_send()

    @pl.when(owns)
    def _():
        for i in range(CHIPS):
            @pl.when(i != chip)
            def _(i=i):
                give(i).wait_send()

    n_swap.wait_send()
    for cp in (relay_r, relay_l, direct_r, direct_l, sum_r, sum_l):
        cp.wait_send()


def on_device(*args):
    any_space = pl.BlockSpec(memory_space=pl.ANY)
    vmem = pl.BlockSpec(memory_space=pltpu.VMEM)
    smem = pl.BlockSpec(memory_space=pltpu.SMEM)
    dma = pltpu.SemaphoreType.DMA
    return pl.pallas_call(
        kernel,
        out_shape=jax.ShapeDtypeStruct((64, DM), BF16),
        in_specs=[any_space] * 7 + [vmem] * 3 + [smem] * 3 + [vmem] + [any_space] * 2,
        out_specs=vmem,
        scratch_shapes=[
            pltpu.VMEM((HALO + ROWS, DM), BF16),
            pltpu.VMEM((6, DM, 256), BF16),
            pltpu.VMEM((DM, 8), BF16),
            pltpu.VMEM((DM, 8), BF16),
            pltpu.VMEM((1024, DM), BF16),
            pltpu.VMEM((128, 128), F32),
            pltpu.VMEM((4, HALO + ROWS, 256), F32),
            pltpu.VMEM((ROWS, 256), BF16),
            pltpu.VMEM((ROWS, 256), BF16),
            pltpu.VMEM((ROWS, 512), F32),
            pltpu.VMEM((ROWS, 512), F32),
            pltpu.VMEM((NC, CH, 128), F32),
            pltpu.VMEM((NC, 8, CH), F32),
            pltpu.VMEM((NC, CH, 128), F32),
            pltpu.VMEM((8, CH, 256), BF16),
            pltpu.VMEM((8, CH, 256), BF16),
            pltpu.VMEM((16, CH, CH), BF16),
            pltpu.VMEM((16, CH, 256), BF16),
            pltpu.VMEM((16, 128, 256), F32),
            pltpu.VMEM((16, 128, 256), BF16),
            pltpu.VMEM((NC, 8, 128), F32),
            pltpu.VMEM((ROWS, 512), BF16),
            pltpu.VMEM((ROWS, 512), F32),
            pltpu.VMEM((8, MSG, 128), BF16),
            pltpu.VMEM((CHIPS, MSG, 128), BF16),
            pltpu.VMEM((CHIPS, 64, 128), BF16),
            pltpu.VMEM((8, 64, 128), BF16),
            pltpu.VMEM((OWN, 512), BF16),
            pltpu.VMEM((2, OWN, 512), BF16),
            pltpu.VMEM((6, 64, 1024), BF16),
            pltpu.VMEM((2, 64, 1024), BF16),
            pltpu.VMEM((4, 64, 1024), BF16),
            pltpu.VMEM((64, DM), F32),
            pltpu.VMEM((2, 64, 1024), F32),
            dma((5,)),
            dma((6,)),
            dma((2,)),
            dma((3,)),
            dma((8,)),
            dma((CHIPS,)),
            dma((CHIPS,)),
            dma((8,)),
            dma((2,)),
            dma((6,)),
            dma((6,)),
        ],
        compiler_params=pltpu.CompilerParams(
            collective_id=0, has_side_effects=True, vmem_limit_bytes=56 * 1024 * 1024
        ),
    )(*args)


def solution(mesh):
    placed = (
        P("seq", None),
        P(None, "head"),
        P(None, "head"),
        P(None, "head"),
        P(None, "head"),
        P(None, "head"),
        P(None, "head"),
        P(None, "head"),
        P(None, "head"),
        P(None, "head"),
        P("head"),
        P("head"),
        P("head"),
        P(),
        P("head", None),
        P("head", None, None),
    )
    return jax.shard_map(
        on_device, mesh=mesh, in_specs=placed, out_specs=P(("seq", "head"), None), check_vma=False
    )
```

time: 854 us -> 61.2 us (0.07)
  the two profiles are of different devices: /device:TPU:24 before, /device:TPU:1 now
where the time goes in v1:
time: 61.2 us; the launch traced here: 60.8 us
  Pallas kernels  55.6 us (91%)
  local copies, waits for them, and re-layouts  5.2 us (8%)
    pallas_call x1, Pallas kernels, on_device(): pl.pallas_call(kernel, out_shape=jax.ShapeDtypeStruct((64, DM), BF16), in...  55.6 us
    unnamed x3, local copies, waits for them, and re-layouts  5.2 us

profile of v1, /device:TPU:1, one launch (start us, length us, event | category | flops | bytes accessed | tf_op | source)
XLA Modules:
  0.0 60.8 jit_solution(11016828966303970642)
XLA Ops:
  0.0 1.8 %copy.17.w_decay = bf16[2048,8]{1,0:T(8,128)(2,1)} copy(bf16[2048,8]{0,1:T(8,128)(2,1)} %param.21) | data formatting | bytes 65536 | tf_op args[5]
  1.8 1.8 %copy.18.w_beta = bf16[2048,8]{1,0:T(8,128)(2,1)} copy(bf16[2048,8]{0,1:T(8,128)(2,1)} %param.22) | data formatting | bytes 65536 | tf_op args[6]
  3.5 55.6 %shard_map.154 = bf16[64,2048]{1,0:T(8,128)(2,1)} custom-call(bf16[256,2048]{1,0:T(8,128)(2,1)} %hidden.1, bf16[2048,512]{1,0:T(8,128)(2,1)} %w_query.1, bf16[2048,512]{1,0:T(8,128)(2,1)} %w_key.1, bf16[2048,1024]{1,0:T(8,128)(2,1)} %w_value.1, bf16[2048,1024]{1,0:T(8,128)(2,1)} %w_gate_z.1, bf16[2048,8]{1,0:T(8,128)(2,1)} %copy.17.w_decay, ...), custom_call_target="tpu_custom_call" | custom-call | tf_op jit(solution)/shard_map/pallas_call | solution.py:468
  59.2 1.7 %copy.20 = bf16[64,2048]{1,0:T(8,128)(2,1)} copy(bf16[64,2048]{1,0:T(8,128)(2,1)} %shard_map.154) | data formatting | bytes 524288

commit v2 on v1

--- a/solution.py
+++ b/solution.py
@@ -16,7 +16,9 @@
 NC = ROWS // CH
 HEADS = 4
 CHIPS = 16
-MSG = 208
+MSG = 272
+LAST = CHIPS - 1
+OWNERS = ((3, 6, 9, 12), (2, 5, 10, 13))
 
 
 def dot(a, b):
@@ -35,9 +37,9 @@
     hidden, w_query, w_key, w_value, w_gate_z, w_decay, w_beta, conv_query, conv_key, conv_value,
     decay_log, decay_bias, beta_bias, norm_gain, w_out, state_in,
     out,
-    hid, wbuf, wdec, wbet, wo, st0, raw, qs, ks, vs, zs, cum, cumt, beta, low, tri, att, uw, ee, sb, ab,
+    hid, wbuf, wo, st0, raw0, raw1, raw2, raw3, qs, ks, vs, zs, cum, cumt, low, tri, att, uw, ee, sb, ab,
     reach, outloc, send, recv, step_out, entering, nsend, nfull, rs_send, rs_relay, rs_arr, rs_own, rs_hold,
-    lsem, wsem, xsem, hsem, msend, mrecv, osend, orecv, nsem, rsend, rrecv,
+    lsem, wsem, xsem, hsem, msend, mrecv, osend, orecv, nsem, rsend, rrecv, ready,
 ):
     seq = lax.axis_index("seq")
     xx = lax.axis_index("head")
@@ -62,11 +64,23 @@
             src_ref=src, dst_ref=dst, send_sem=s_sem, recv_sem=r_sem, device_id=device, device_id_type=MESH
         )
 
-    mine = pl.ds(pl.multiple_of(HALO + core * OWN, 16), OWN)
-    theirs = pl.ds(pl.multiple_of(HALO + other * OWN, 16), OWN)
     col256 = pl.ds(pl.multiple_of(core * 256, 256), 256)
-
-    own_copy = local(hidden, hid.at[mine, :], lsem.at[0])
+    owners = [lax.select(core == 0, OWNERS[0][j], OWNERS[1][j]) for j in range(HEADS)]
+    my_head = jnp.int32(0)
+    owns = owners[0] == chip
+    for j in range(1, HEADS):
+        my_head = lax.select(owners[j] == chip, j, my_head)
+        owns = owns | (owners[j] == chip)
+    owns_one = lax.select(owns, 1, 0)
+
+    def chunk_rows(c):
+        return pl.ds(c * CH, CH)
+
+    def run(step):
+        for c in range(NC):
+            step(c, 0)
+
+    own_copy = local(hidden, hid.at[pl.ds(0, OWN), :], lsem.at[0])
     own_copy.start()
     w_copies = [
         local(w_query.at[:, col256], wbuf.at[0], wsem.at[0]),
@@ -78,20 +92,10 @@
     for i in range(2):
         cols = pl.ds(pl.multiple_of(core * 512 + i * 256, 256), 256)
         w_copies.append(local(w_gate_z.at[:, cols], wbuf.at[4 + i], wsem.at[4 + i]))
-    dec_copy = local(w_decay, wdec, lsem.at[1])
-    bet_copy = local(w_beta, wbet, lsem.at[2])
-    for cp in w_copies[:2]:
+    for cp in w_copies[:4]:
         cp.start()
-    dec_copy.start()
-    bet_copy.start()
-    for cp in w_copies[2:]:
-        cp.start()
-    owner_head = core * HEADS + chip // 4
-    owner_slot = chip // 2
-    st_copy = local(state_in.at[owner_head], st0, lsem.at[3])
-    st_copy.start()
+    st_copy = local(state_in.at[core * HEADS + my_head], st0, lsem.at[3])
     wo_copy = local(w_out, wo, lsem.at[4])
-    wo_copy.start()
 
     barrier = pltpu.get_barrier_semaphore()
 
@@ -99,35 +103,63 @@
         pl.semaphore_signal(barrier, inc=1, device_id=device, device_id_type=MESH)
 
     greet(partner)
-    greet((lax.select(core == 1, nxt * 2, prv * 2 + 1), xx))
     greet(at_x(right))
     greet(at_x(left))
 
-    def greet_chip(k, carry):
-        greet((lax.rem(chip + k, CHIPS) * 2 + core, xx))
-        return carry
-
-    lax.fori_loop(1, CHIPS, greet_chip, 0)
-    pl.semaphore_wait(barrier, 19)
-
-    swap = remote(hidden, hid.at[mine, :], xsem.at[0], xsem.at[1], partner)
+    @pl.when(chip > 0)
+    def _():
+        greet((prv * 2 + 1, xx))
+
+    @pl.when(owns)
+    def _():
+        def greet_chip(k, carry):
+            greet((lax.rem(chip + k, CHIPS) * 2 + core, xx))
+            return carry
+
+        lax.fori_loop(1, CHIPS, greet_chip, 0)
+
+    sends_halo = (core == 1) & (chip < LAST)
+    pl.semaphore_wait(barrier, 3 + HEADS - owns_one + lax.select(sends_halo, 2, 0))
+
+    swap = remote(hidden, hid.at[pl.ds(OWN, OWN), :], xsem.at[0], xsem.at[1], partner)
     swap.start()
     tail = hidden.at[pl.ds(OWN - HALO, HALO), :]
-    halo0 = remote(tail, hid.at[pl.ds(0, HALO), :], hsem.at[0], hsem.at[2], (nxt * 2, xx))
-    halo1 = remote(tail, hid.at[pl.ds(0, HALO), :], hsem.at[1], hsem.at[2], (nxt * 2 + 1, xx))
-
-    @pl.when(core == 1)
+    halo_at = hid.at[pl.ds(ROWS, HALO), :]
+    halo0 = remote(tail, halo_at, hsem.at[0], hsem.at[2], (nxt * 2, xx))
+    halo1 = remote(tail, halo_at, hsem.at[1], hsem.at[2], (nxt * 2 + 1, xx))
+
+    @pl.when(sends_halo)
     def _():
         halo0.start()
         halo1.start()
 
+    for j in range(HEADS):
+        @pl.when(owners[j] != chip)
+        def _(j=j):
+            pl.semaphore_signal(
+                ready.at[chip], inc=1, device_id=(owners[j] * 2 + core, xx), device_id_type=MESH
+            )
+
+    raws = (raw0, raw1, raw2, raw3)
+    rows_own = pl.ds(pl.multiple_of(HALO + core * OWN, 16), OWN)
+    rows_other = pl.ds(pl.multiple_of(HALO + other * OWN, 16), OWN)
     own_copy.wait()
+    for b in range(4):
+        w_copies[b].wait()
+        raws[b][rows_own, :] = dot(hid[0:OWN, :], wbuf[b]).astype(BF16).astype(F32)
+    for cp in w_copies[4:]:
+        cp.start()
+    st_copy.start()
+    wo_copy.start()
     swap.wait_recv()
-    halo0.wait_recv()
+
+    @pl.when(chip > 0)
+    def _():
+        halo0.wait_recv()
 
     @pl.when(chip == 0)
     def _():
-        hid[pl.ds(0, HALO), :] = jnp.zeros((HALO, DM), BF16)
+        hid[ROWS : ROWS + HALO, :] = jnp.zeros((HALO, DM), BF16)
 
     taps_of = (
         lambda: conv_query[:, col256].astype(F32),
@@ -136,19 +168,15 @@
         lambda: conv_value[:, pl.ds(pl.multiple_of(core * 512 + 256, 256), 256)].astype(F32),
     )
     for b in range(4):
-        w_copies[b].wait()
-
-        def rows_of(t, carry, b=b):
-            r = pl.ds(pl.multiple_of(t * 176, 16), 176)
-            raw[b, r, :] = dot(hid[r, :], wbuf[b]).astype(BF16).astype(F32)
-            return carry
-
-        lax.fori_loop(0, 3, rows_of, 0)
+        raw = raws[b]
+        rest = dot(hid[OWN : ROWS + HALO, :], wbuf[b]).astype(BF16).astype(F32)
+        raw[rows_other, :] = rest[:OWN]
+        raw[0:HALO, :] = rest[OWN:]
         taps = taps_of[b]()
         for t in range(NC):
             pre = jnp.zeros((CH, 256), F32)
             for i in range(4):
-                pre = pre + taps[i : i + 1, :] * raw[b, pl.ds(HALO - 3 + i + t * CH, CH), :]
+                pre = pre + taps[i : i + 1, :] * raw[pl.ds(HALO - 3 + i + t * CH, CH), :]
             act = silu(pre)
             r = pl.ds(t * CH, CH)
             if b < 2:
@@ -162,42 +190,40 @@
             else:
                 vs[r, (b - 2) * 256 : (b - 1) * 256] = act
 
-    dec_copy.wait()
-    bet_copy.wait()
-    lane = lax.broadcasted_iota(jnp.int32, (1, HEADS), 1)
-
-    def lanes_of(ref):
-        v = jnp.zeros((1, HEADS), F32)
+    head_row = lax.broadcasted_iota(jnp.int32, (HEADS, 1), 0)
+
+    def column_of(ref):
+        v = jnp.zeros((HEADS, 1), F32)
         for h in range(HEADS):
-            v = jnp.where(lane == h, ref[core * HEADS + h], v)
+            v = jnp.where(head_row == h, ref[core * HEADS + h], v)
         return v
 
-    rate = -jnp.exp(lanes_of(decay_log))
-    d_bias = lanes_of(decay_bias)
-    b_bias = lanes_of(beta_bias)
+    rate = -jnp.exp(column_of(decay_log))
     ti = lax.broadcasted_iota(jnp.int32, (CH, CH), 0)
     tj = lax.broadcasted_iota(jnp.int32, (CH, CH), 1)
     incl = ti >= tj
-    ones_low = jnp.where(incl, 1.0, 0.0).astype(F32)
+    ones_up = jnp.where(ti <= tj, 1.0, 0.0).astype(F32)
+    w_gates = jnp.concatenate([w_decay[...].astype(F32), w_beta[...].astype(F32)], 0).astype(BF16)
+    lg = dot_nt(w_gates, hid[0:ROWS, :])
+    logits = jnp.concatenate(
+        [jnp.where(core == 0, lg[:, :OWN], lg[:, OWN:]), jnp.where(core == 0, lg[:, OWN:], lg[:, :OWN])], 1
+    )
+    u = jnp.where(core == 0, logits[0:4], logits[4:8]) + column_of(decay_bias)
+    glog = rate * (jnp.maximum(u, 0.0) + jnp.log1p(jnp.exp(-jnp.abs(u))))
+    strength = jax.nn.sigmoid(jnp.where(core == 0, logits[8:12], logits[12:16]) + column_of(beta_bias))
+    pad4 = jnp.zeros((4, CH), F32)
     for t in range(NC):
-        hrows = hid[pl.ds(HALO + t * CH, CH), :]
-        gd = dot(hrows, wdec[...])
-        gb = dot(hrows, wbet[...])
-        gd = jnp.where(core == 0, gd[:, :HEADS], gd[:, HEADS:])
-        gb = jnp.where(core == 0, gb[:, :HEADS], gb[:, HEADS:])
-        u = gd + d_bias
-        soft = jnp.maximum(u, 0.0) + jnp.log1p(jnp.exp(-jnp.abs(u)))
-        glog = jnp.concatenate([rate * soft, jnp.zeros((CH, 128 - HEADS), F32)], 1)
-        cm = jnp.dot(ones_low, glog, precision=lax.Precision.HIGHEST, preferred_element_type=F32)
-        cum[t] = cm
-        cumt[t] = cm.T[:8, :]
-        beta[t] = jnp.concatenate([jax.nn.sigmoid(gb + b_bias), jnp.zeros((CH, 128 - HEADS), F32)], 1)
+        cols = slice(t * CH, (t + 1) * CH)
+        g8 = jnp.concatenate([glog[:, cols], pad4], 0)
+        cr8 = jnp.dot(g8, ones_up, precision=lax.Precision.HIGHEST, preferred_element_type=F32)
+        cumt[t] = cr8
+        stacked = jnp.concatenate([cr8, strength[:, cols], jnp.zeros((CH - 12, CH), F32)], 0)
+        cum[t] = stacked.T
 
     def systems(c, carry):
-        r = pl.ds(pl.multiple_of(c * CH, CH), CH)
+        r = chunk_rows(c)
         cc_all = cum[c]
         cr_all = cumt[c]
-        be_all = beta[c]
         for g in range(2):
             k = ks[r, g * 128 : (g + 1) * 128]
             q = qs[r, g * 128 : (g + 1) * 128]
@@ -207,7 +233,7 @@
                 h = 2 * g + e
                 diff = cc_all[:, h : h + 1] - cr_all[h : h + 1, :]
                 ratio = jnp.exp(jnp.where(incl, diff, -1e30))
-                lo = jnp.where(ti > tj, be_all[:, h : h + 1] * ratio * kk, 0.0)
+                lo = jnp.where(ti > tj, cc_all[:, 8 + h : 9 + h] * ratio * kk, 0.0)
                 low[c * 2 + g, :, e * 128 : (e + 1) * 128] = lo.astype(BF16)
                 att[c * 4 + h] = (ratio * qk).astype(BF16)
                 tri[c * 2 + g, :, e * 128 : (e + 1) * 128] = jnp.where(
@@ -215,7 +241,7 @@
                 ).astype(BF16)
         return carry
 
-    lax.fori_loop(0, NC, systems, 0)
+    run(systems)
 
     z128 = jnp.zeros((CH, CH), BF16)
 
@@ -243,16 +269,15 @@
     lax.fori_loop(0, 6, double, jnp.int32(2))
 
     def unit(c, carry):
-        r = pl.ds(pl.multiple_of(c * CH, CH), CH)
+        r = chunk_rows(c)
         cc_all = cum[c]
         cr_all = cumt[c]
-        be_all = beta[c]
         for g in range(2):
             k = ks[r, g * 128 : (g + 1) * 128].astype(F32)
             kt = k.T
             for e in range(2):
                 h = 2 * g + e
-                be = be_all[:, h : h + 1]
+                be = cc_all[:, 8 + h : 9 + h]
                 cc = cc_all[:, h : h + 1]
                 cr = cr_all[h : h + 1, :]
                 tail_w = jnp.exp(cr[:, 127:128] - cr)
@@ -262,7 +287,7 @@
                 ee[c * 4 + h] = dot((kt * tail_w).astype(BF16), u)
         return carry
 
-    lax.fori_loop(0, NC, unit, 0)
+    run(unit)
 
     row16 = lax.broadcasted_iota(jnp.int32, (16, 128), 0)
     s_cur, b_cur, a_cur = [], [], []
@@ -292,26 +317,24 @@
         a_full = jnp.broadcast_to(a_cur[h], (16, 128))
         a_hi = a_full.astype(BF16).astype(F32)
         a_rows = jnp.where(row16 < 8, a_hi, a_full - a_hi).astype(BF16)
-        for half in range(2):
-            o = 2 * h + half
-            send[o, 0:128, :] = bt
-            send[o, 128:192, :] = s_t[half * 64 : (half + 1) * 64, :]
-            send[o, 192:208, :] = a_rows
-
-    def to_owner(o):
-        return remote(send.at[o], recv.at[chip], msend.at[o], mrecv.at[chip], ((2 * o + core) * 2 + core, xx))
-
-    for o in range(8):
-        @pl.when(2 * o + core != chip)
-        def _(o=o):
-            to_owner(o).start()
-
-        @pl.when(2 * o + core == chip)
-        def _(o=o):
-            recv[chip] = send[o]
+        send[h, 0:128, :] = bt
+        send[h, 128:256, :] = s_t
+        send[h, 256:272, :] = a_rows
+
+    def to_owner(j):
+        return remote(send.at[j], recv.at[chip], msend.at[j], mrecv.at[chip], (owners[j] * 2 + core, xx))
+
+    for j in range(HEADS):
+        @pl.when((owners[j] != chip) & (chip < LAST))
+        def _(j=j):
+            to_owner(j).start()
+
+        @pl.when(owners[j] == chip)
+        def _(j=j):
+            recv[chip] = send[j]
 
     def local_part(c, carry):
-        r = pl.ds(pl.multiple_of(c * CH, CH), CH)
+        r = chunk_rows(c)
         cc_all = cum[c]
         a_all = ab[c]
         for h in range(HEADS):
@@ -324,61 +347,60 @@
             reach[r, h * 128 : (h + 1) * 128] = (a_all[h : h + 1, :] * qeff + rr[:, 128:]).astype(BF16)
         return carry
 
-    lax.fori_loop(0, NC, local_part, 0)
-
-    owns = lax.rem(chip, 2) == core
+    run(local_part)
+
+    for b in range(2):
+        w_copies[4 + b].wait()
+    gain = jnp.concatenate([norm_gain[...].reshape(1, 128)] * 2, 1)
+
+    def gate_rows(t, carry):
+        r = chunk_rows(t)
+        h_rows = hid[chunk_rows(t), :]
+        for b in range(2):
+            zs[r, b * 256 : (b + 1) * 256] = silu(dot(h_rows, wbuf[4 + b])) * gain
+        return carry
+
+    run(gate_rows)
+
     st_copy.wait()
 
     def give(i):
-        return remote(step_out.at[i], entering.at[owner_slot], osend.at[i], orecv.at[owner_slot], (i * 2 + core, xx))
+        return remote(step_out.at[i], entering.at[my_head], osend.at[i], orecv.at[my_head], (i * 2 + core, xx))
 
     @pl.when(owns)
     def _():
-        for i in range(CHIPS):
-            @pl.when(i != chip)
-            def _(i=i):
-                remote(send.at[0], recv.at[i], msend.at[0], mrecv.at[i], partner).wait_recv()
-        st_t = st0[...].T
-        s = jnp.where(lax.rem(owner_slot, 2) == 0, st_t[:64], st_t[64:])
+        s = st0[...].T
         for i in range(CHIPS):
             sbf = s.astype(BF16)
             step_out[i] = sbf
 
             @pl.when(i != chip)
             def _(i=i):
+                pl.semaphore_wait(ready.at[i], 1)
                 give(i).start()
 
-            if i < CHIPS - 1:
-                a = recv[i, 192:208, :].astype(F32)
-                s = (a[0:1, :] + a[8:9, :]) * s + dot(sbf, recv[i, 0:128, :]) + recv[i, 128:192, :].astype(F32)
-        entering[owner_slot] = step_out[chip]
-
-    for b in range(2):
-        w_copies[4 + b].wait()
-    gain = jnp.concatenate([norm_gain[...].reshape(1, 128)] * 2, 1)
-
-    def gate_rows(t, carry):
-        r = pl.ds(pl.multiple_of(t * CH, CH), CH)
-        h_rows = hid[pl.ds(pl.multiple_of(HALO + t * CH, 16), CH), :]
-        for b in range(2):
-            zs[r, b * 256 : (b + 1) * 256] = silu(dot(h_rows, wbuf[4 + b])) * gain
-        return carry
-
-    lax.fori_loop(0, NC, gate_rows, 0)
-
-    for o in range(8):
-        @pl.when(2 * o + core != chip)
-        def _(o=o):
-            remote(step_out.at[0], entering.at[o], osend.at[0], orecv.at[o], partner).wait_recv()
-
-    def finish(base, put):
+            if i < LAST:
+                @pl.when(i != chip)
+                def _(i=i):
+                    remote(send.at[0], recv.at[i], msend.at[0], mrecv.at[i], partner).wait_recv()
+
+                a = recv[i, 256:272, :].astype(F32)
+                s = (a[0:1, :] + a[8:9, :]) * s + dot(sbf, recv[i, 0:128, :]) + recv[i, 128:256, :].astype(F32)
+        entering[my_head] = step_out[chip]
+
+    for j in range(HEADS):
+        @pl.when(owners[j] != chip)
+        def _(j=j):
+            remote(step_out.at[0], entering.at[j], osend.at[0], orecv.at[j], partner).wait_recv()
+
+    def finish(base, z_base, put):
         for t in range(2):
             r = pl.ds(pl.multiple_of(base + t * CH, CH), CH)
             for h in range(HEADS):
                 cols = slice(h * 128, (h + 1) * 128)
-                s_t = jnp.concatenate([entering[2 * h], entering[2 * h + 1]], 0)
+                s_t = entering[h]
                 o = outloc[r, cols] + dot_nt(reach[r, cols], s_t)
-                n = o * lax.rsqrt(jnp.mean(o * o, axis=-1, keepdims=True) + 1e-6) * zs[r, cols]
+                n = o * lax.rsqrt(jnp.mean(o * o, axis=-1, keepdims=True) + 1e-6) * zs[z_base + t * CH : z_base + (t + 1) * CH, cols]
                 put(t, cols, n.astype(BF16))
 
     def put_send(t, cols, v):
@@ -387,10 +409,10 @@
     def put_own(t, cols, v):
         nfull[core, t * CH : (t + 1) * CH, cols] = v
 
-    finish(other * OWN, put_send)
+    finish(other * OWN, OWN, put_send)
     n_swap = remote(nsend, nfull.at[core], nsem.at[0], nsem.at[1], partner)
     n_swap.start()
-    finish(core * OWN, put_own)
+    finish(core * OWN, 0, put_own)
     wo_copy.wait()
     n_swap.wait_recv()
 
@@ -438,15 +460,15 @@
 
     swap.wait_send()
 
-    @pl.when(core == 1)
+    @pl.when(sends_halo)
     def _():
         halo0.wait_send()
         halo1.wait_send()
 
-    for o in range(8):
-        @pl.when(2 * o + core != chip)
-        def _(o=o):
-            to_owner(o).wait_send()
+    for j in range(HEADS):
+        @pl.when((owners[j] != chip) & (chip < LAST))
+        def _(j=j):
+            to_owner(j).wait_send()
 
     @pl.when(owns)
     def _():
@@ -468,23 +490,20 @@
     return pl.pallas_call(
         kernel,
         out_shape=jax.ShapeDtypeStruct((64, DM), BF16),
-        in_specs=[any_space] * 7 + [vmem] * 3 + [smem] * 3 + [vmem] + [any_space] * 2,
+        in_specs=[any_space] * 5 + [vmem] * 5 + [smem] * 3 + [vmem] + [any_space] * 2,
         out_specs=vmem,
         scratch_shapes=[
             pltpu.VMEM((HALO + ROWS, DM), BF16),
             pltpu.VMEM((6, DM, 256), BF16),
-            pltpu.VMEM((DM, 8), BF16),
-            pltpu.VMEM((DM, 8), BF16),
             pltpu.VMEM((1024, DM), BF16),
             pltpu.VMEM((128, 128), F32),
-            pltpu.VMEM((4, HALO + ROWS, 256), F32),
+            *[pltpu.VMEM((HALO + ROWS, 256), F32)] * 4,
             pltpu.VMEM((ROWS, 256), BF16),
             pltpu.VMEM((ROWS, 256), BF16),
             pltpu.VMEM((ROWS, 512), F32),
             pltpu.VMEM((ROWS, 512), F32),
             pltpu.VMEM((NC, CH, 128), F32),
             pltpu.VMEM((NC, 8, CH), F32),
-            pltpu.VMEM((NC, CH, 128), F32),
             pltpu.VMEM((8, CH, 256), BF16),
             pltpu.VMEM((8, CH, 256), BF16),
             pltpu.VMEM((16, CH, CH), BF16),
@@ -494,10 +513,10 @@
             pltpu.VMEM((NC, 8, 128), F32),
             pltpu.VMEM((ROWS, 512), BF16),
             pltpu.VMEM((ROWS, 512), F32),
-            pltpu.VMEM((8, MSG, 128), BF16),
+            pltpu.VMEM((HEADS, MSG, 128), BF16),
             pltpu.VMEM((CHIPS, MSG, 128), BF16),
-            pltpu.VMEM((CHIPS, 64, 128), BF16),
-            pltpu.VMEM((8, 64, 128), BF16),
+            pltpu.VMEM((CHIPS, 128, 128), BF16),
+            pltpu.VMEM((HEADS, 128, 128), BF16),
             pltpu.VMEM((OWN, 512), BF16),
             pltpu.VMEM((2, OWN, 512), BF16),
             pltpu.VMEM((6, 64, 1024), BF16),
@@ -509,18 +528,19 @@
             dma((6,)),
             dma((2,)),
             dma((3,)),
-            dma((8,)),
+            dma((HEADS,)),
             dma((CHIPS,)),
             dma((CHIPS,)),
-            dma((8,)),
+            dma((HEADS,)),
             dma((2,)),
             dma((6,)),
             dma((6,)),
+            pltpu.SemaphoreType.REGULAR((CHIPS,)),
         ],
         compiler_params=pltpu.CompilerParams(
             collective_id=0, has_side_effects=True, vmem_limit_bytes=56 * 1024 * 1024
         ),
-    )(*args)
+    )(*args[:5], args[5].T, args[6].T, *args[7:])
 
 
 def solution(mesh):

time: 61.2 us -> 51 us (0.83)
  the two profiles are of different devices: /device:TPU:1 before, /device:TPU:24 now
where the time goes in v2:
time: 51 us; the launch traced here: 50.5 us
  Pallas kernels  48.8 us (96%)
  local copies, waits for them, and re-layouts  1.67 us (3%)
    pallas_call x1, Pallas kernels, on_device(): pl.pallas_call(kernel, out_shape=jax.ShapeDtypeStruct((64, DM), BF16), in...  48.8 us
    unnamed x1, local copies, waits for them, and re-layouts  1.67 us

profile of v2, /device:TPU:24, one launch (start us, length us, event | category | flops | bytes accessed | tf_op | source)
XLA Modules:
  0.0 50.5 jit_solution(11128511900003397196)
XLA Ops:
  0.0 48.8 %shard_map.154 = bf16[64,2048]{1,0:T(8,128)(2,1)} custom-call(bf16[256,2048]{1,0:T(8,128)(2,1)} %hidden.1, bf16[2048,512]{1,0:T(8,128)(2,1)} %w_query.1, bf16[2048,512]{1,0:T(8,128)(2,1)} %w_key.1, bf16[2048,1024]{1,0:T(8,128)(2,1)} %w_value.1, bf16[2048,1024]{1,0:T(8,128)(2,1)} %w_gate_z.1, bf16[8,2048]{1,0:T(8,128)(2,1)} %bitcast.2, ...), custom_call_target="tpu_custom_call" | custom-call | tf_op jit(solution)/shard_map/pallas_call | solution.py:490
  48.8 1.7 %copy.18 = bf16[64,2048]{1,0:T(8,128)(2,1)} copy(bf16[64,2048]{1,0:T(8,128)(2,1)} %shard_map.154) | data formatting | bytes 524288

commit v3 on v2

v3 whole, which is shorter than its diff:
```python
import jax
import jax.numpy as jnp
from jax import lax
from jax.experimental import pallas as pl
from jax.experimental.pallas import tpu as pltpu
from jax.sharding import PartitionSpec as P

MESH = pl.DeviceIdType.MESH
F32 = jnp.float32
BF16 = jnp.bfloat16
HALO = 16
OWN = 256
ROWS = 512
DM = 2048
CH = 128
NC = ROWS // CH
HEADS = 4
CHIPS = 16
MSG = 272
LAST = CHIPS - 1
LINE = 4


def dot(a, b):
    return jnp.dot(a, b, preferred_element_type=F32)


def dot_nt(a, b):
    return lax.dot_general(a, b, (((1,), (1,)), ((), ())), preferred_element_type=F32)


def silu(u):
    return u * jax.nn.sigmoid(u)


def kernel(
    hidden, w_query, w_key, w_value, w_gate_z, w_decay, w_beta, conv_query, conv_key, conv_value,
    decay_log, decay_bias, beta_bias, norm_gain, w_out, state_in,
    out,
    hid, wbuf, wo, st0, raw0, raw1, raw2, raw3, qs, ks, vs, zs, cum, cumt, low, tri, att, uw, ee, sb, ab,
    reach, outloc, send, recv, tsend, trecv, pre_x, pre_a, step_out, entering, nsend, nfull, rs_send, rs_relay, rs_arr, rs_own, rs_hold,
    lsem, wsem, xsem, hsem, msend, mrecv, tsems, osend, orecv, nsem, rsend, rrecv, ready,
):
    seq = lax.axis_index("seq")
    xx = lax.axis_index("head")
    chip = seq // 2
    core = seq % 2
    other = 1 - core
    partner = (chip * 2 + other, xx)
    nxt = lax.rem(chip + 1, CHIPS)
    prv = lax.rem(chip + CHIPS - 1, CHIPS)
    right = lax.rem(xx + 1, 4)
    left = lax.rem(xx + 3, 4)
    across = lax.rem(xx + 2, 4)

    def at_x(x):
        return (seq, x)

    def local(src, dst, sem):
        return pltpu.make_async_copy(src, dst, sem)

    def remote(src, dst, s_sem, r_sem, device):
        return pltpu.make_async_remote_copy(
            src_ref=src, dst_ref=dst, send_sem=s_sem, recv_sem=r_sem, device_id=device, device_id_type=MESH
        )

    col256 = pl.ds(pl.multiple_of(core * 256, 256), 256)
    zz = lax.rem(chip, LINE)
    yy = chip // LINE

    def at_z(z):
        return ((yy * LINE + z) * 2 + core, xx)

    def at_y(y):
        return ((y * LINE + zz) * 2 + core, xx)

    def chunk_rows(c):
        return pl.ds(c * CH, CH)

    def run(step):
        for c in range(NC):
            step(c, 0)

    own_copy = local(hidden, hid.at[pl.ds(0, OWN), :], lsem.at[0])
    own_copy.start()
    w_copies = [
        local(w_query.at[:, col256], wbuf.at[0], wsem.at[0]),
        local(w_key.at[:, col256], wbuf.at[1], wsem.at[1]),
    ]
    for i in range(2):
        cols = pl.ds(pl.multiple_of(core * 512 + i * 256, 256), 256)
        w_copies.append(local(w_value.at[:, cols], wbuf.at[2 + i], wsem.at[2 + i]))
    for i in range(2):
        cols = pl.ds(pl.multiple_of(core * 512 + i * 256, 256), 256)
        w_copies.append(local(w_gate_z.at[:, cols], wbuf.at[4 + i], wsem.at[4 + i]))
    for cp in w_copies[:4]:
        cp.start()
    st_copy = local(state_in.at[core * HEADS + zz], st0, lsem.at[3])
    wo_copy = local(w_out, wo, lsem.at[4])

    barrier = pltpu.get_barrier_semaphore()

    def greet(device):
        pl.semaphore_signal(barrier, inc=1, device_id=device, device_id_type=MESH)

    greet(partner)
    greet(at_x(right))
    greet(at_x(left))

    @pl.when(chip > 0)
    def _():
        greet((prv * 2 + 1, xx))

    for n in range(1, LINE):
        @pl.when(n > zz)
        def _(n=n):
            greet(at_z(n))

        @pl.when(n > yy)
        def _(n=n):
            greet(at_y(n))

    sends_halo = (core == 1) & (chip < LAST)
    pl.semaphore_wait(barrier, 3 + zz + yy + lax.select(sends_halo, 2, 0))

    swaps = [
        remote(
            hidden.at[pl.ds(i * 64, 64), :], hid.at[pl.ds(OWN + i * 64, 64), :], xsem.at[i], xsem.at[4 + i], partner
        )
        for i in range(4)
    ]
    for cp in swaps:
        cp.start()
    tail = hidden.at[pl.ds(OWN - HALO, HALO), :]
    halo_at = hid.at[pl.ds(ROWS, HALO), :]
    halo0 = remote(tail, halo_at, hsem.at[0], hsem.at[2], (nxt * 2, xx))
    halo1 = remote(tail, halo_at, hsem.at[1], hsem.at[2], (nxt * 2 + 1, xx))

    @pl.when(sends_halo)
    def _():
        halo0.start()
        halo1.start()

    for n in range(LINE - 1):
        @pl.when(n < zz)
        def _(n=n):
            pl.semaphore_signal(ready.at[zz], inc=1, device_id=at_z(n), device_id_type=MESH)

        @pl.when(n < yy)
        def _(n=n):
            pl.semaphore_signal(ready.at[LINE + yy], inc=1, device_id=at_y(n), device_id_type=MESH)

    raws = (raw0, raw1, raw2, raw3)
    rows_own = pl.ds(pl.multiple_of(HALO + core * OWN, 16), OWN)
    rows_other = pl.ds(pl.multiple_of(HALO + other * OWN, 16), OWN)
    own_copy.wait()
    for b in range(4):
        w_copies[b].wait()
        raws[b][rows_own, :] = dot(hid[0:OWN, :], wbuf[b]).astype(BF16).astype(F32)
    for cp in w_copies[4:]:
        cp.start()
    st_copy.start()
    wo_copy.start()
    for cp in swaps:
        cp.wait_recv()

    @pl.when(chip > 0)
    def _():
        halo0.wait_recv()

    @pl.when(chip == 0)
    def _():
        hid[ROWS : ROWS + HALO, :] = jnp.zeros((HALO, DM), BF16)

    taps_of = (
        lambda: conv_query[:, col256].astype(F32),
        lambda: conv_key[:, col256].astype(F32),
        lambda: conv_value[:, pl.ds(pl.multiple_of(core * 512, 256), 256)].astype(F32),
        lambda: conv_value[:, pl.ds(pl.multiple_of(core * 512 + 256, 256), 256)].astype(F32),
    )
    for b in range(4):
        raw = raws[b]
        rest = dot(hid[OWN : ROWS + HALO, :], wbuf[b]).astype(BF16).astype(F32)
        raw[rows_other, :] = rest[:OWN]
        raw[0:HALO, :] = rest[OWN:]
        taps = taps_of[b]()
        for t in range(NC):
            pre = jnp.zeros((CH, 256), F32)
            for i in range(4):
                pre = pre + taps[i : i + 1, :] * raw[pl.ds(HALO - 3 + i + t * CH, CH), :]
            act = silu(pre)
            r = pl.ds(t * CH, CH)
            if b < 2:
                for g in range(2):
                    a = act[:, g * 128 : (g + 1) * 128]
                    n = a * lax.rsqrt(jnp.sum(a * a, axis=-1, keepdims=True) + 1e-6)
                    if b == 0:
                        qs[r, g * 128 : (g + 1) * 128] = (n * 128 ** (-0.5)).astype(BF16)
                    else:
                        ks[r, g * 128 : (g + 1) * 128] = n.astype(BF16)
            else:
                vs[r, (b - 2) * 256 : (b - 1) * 256] = act

    head_row = lax.broadcasted_iota(jnp.int32, (HEADS, 1), 0)

    def column_of(ref):
        v = jnp.zeros((HEADS, 1), F32)
        for h in range(HEADS):
            v = jnp.where(head_row == h, ref[core * HEADS + h], v)
        return v

    rate = -jnp.exp(column_of(decay_log))
    ti = lax.broadcasted_iota(jnp.int32, (CH, CH), 0)
    tj = lax.broadcasted_iota(jnp.int32, (CH, CH), 1)
    incl = ti >= tj
    ones_up = jnp.where(ti <= tj, 1.0, 0.0).astype(F32)
    w_gates = jnp.concatenate([w_decay[...].astype(F32), w_beta[...].astype(F32)], 0).astype(BF16)
    lg = dot_nt(w_gates, hid[0:ROWS, :])
    logits = jnp.concatenate(
        [jnp.where(core == 0, lg[:, :OWN], lg[:, OWN:]), jnp.where(core == 0, lg[:, OWN:], lg[:, :OWN])], 1
    )
    u = jnp.where(core == 0, logits[0:4], logits[4:8]) + column_of(decay_bias)
    glog = rate * (jnp.maximum(u, 0.0) + jnp.log1p(jnp.exp(-jnp.abs(u))))
    strength = jax.nn.sigmoid(jnp.where(core == 0, logits[8:12], logits[12:16]) + column_of(beta_bias))
    pad4 = jnp.zeros((4, CH), F32)
    for t in range(NC):
        cols = slice(t * CH, (t + 1) * CH)
        g8 = jnp.concatenate([glog[:, cols], pad4], 0)
        cr8 = jnp.dot(g8, ones_up, precision=lax.Precision.HIGHEST, preferred_element_type=F32)
        cumt[t] = cr8
        stacked = jnp.concatenate([cr8, strength[:, cols], jnp.zeros((CH - 12, CH), F32)], 0)
        cum[t] = stacked.T

    z128 = jnp.zeros((CH, CH), BF16)

    def pair_diag(m):
        return jnp.concatenate(
            [jnp.concatenate([m[:, :128], z128], 1), jnp.concatenate([z128, m[:, 128:]], 1)], 0
        )

    pi = lax.broadcasted_iota(jnp.int32, (CH, 256), 0)
    pj = lax.broadcasted_iota(jnp.int32, (CH, 256), 1) % 128
    pxor = pi ^ pj
    row16 = lax.broadcasted_iota(jnp.int32, (16, 128), 0)

    def systems(c, g):
        r = chunk_rows(c)
        cc_all = cum[c]
        cr_all = cumt[c]
        k = ks[r, g * 128 : (g + 1) * 128]
        q = qs[r, g * 128 : (g + 1) * 128]
        both = dot_nt(jnp.concatenate([k, q], 0), k)
        kk, qk = both[:CH], both[CH:]
        for e in range(2):
            h = 2 * g + e
            diff = cc_all[:, h : h + 1] - cr_all[h : h + 1, :]
            ratio = jnp.exp(jnp.where(incl, diff, -1e30))
            lo = jnp.where(ti > tj, cc_all[:, 8 + h : 9 + h] * ratio * kk, 0.0)
            low[c * 2 + g, :, e * 128 : (e + 1) * 128] = lo.astype(BF16)
            att[c * 4 + h] = (ratio * qk).astype(BF16)
            tri[c * 2 + g, :, e * 128 : (e + 1) * 128] = jnp.where(
                ti == tj, 1.0, jnp.where((ti ^ tj) == 1, -lo, 0.0)
            ).astype(BF16)

    def invert():
        pairs = range(2 * NC)

        def double(level, size):
            mask = (pxor >= size) & (pxor < 2 * size)
            prods = []
            for p in pairs:
                lm = jnp.where(mask, low[p].astype(F32), 0.0).astype(BF16)
                prods.append(dot(tri[p], pair_diag(lm)).astype(BF16))
            for p, prod in zip(pairs, prods):
                t_old = tri[p]
                y = dot(prod, pair_diag(t_old))
                tri[p] = (t_old.astype(F32) - y).astype(BF16)
            return size * 2

        lax.fori_loop(0, 6, double, jnp.int32(2))

    def unit(c, g):
        r = chunk_rows(c)
        cc_all = cum[c]
        cr_all = cumt[c]
        k = ks[r, g * 128 : (g + 1) * 128].astype(F32)
        kt = k.T
        for e in range(2):
            h = 2 * g + e
            be = cc_all[:, 8 + h : 9 + h]
            cc = cc_all[:, h : h + 1]
            cr = cr_all[h : h + 1, :]
            tail_w = jnp.exp(cr[:, 127:128] - cr)
            rhs = jnp.concatenate([be * vs[r, h * 128 : (h + 1) * 128], (be * jnp.exp(cc)) * k], 1)
            u = dot(tri[c * 2 + g, :, e * 128 : (e + 1) * 128], rhs.astype(BF16)).astype(BF16)
            uw[c * 4 + h] = u
            ee[c * 4 + h] = dot((kt * tail_w).astype(BF16), u)

    def map_of(heads):
        s_cur, b_cur, a_cur = {}, {}, {}
        for h in heads:
            e0 = ee[h]
            s_cur[h] = e0[:, :128]
            b_cur[h] = -e0[:, 128:]
            a_cur[h] = jnp.exp(cumt[0, h : h + 1, 127:128])
            sb[h] = jnp.zeros((128, 256), BF16)
            ab[0, h : h + 1, :] = jnp.ones((1, 128), F32)
        for c in range(1, NC):
            for h in heads:
                s, bm, a = s_cur[h], b_cur[h], a_cur[h]
                packed = jnp.concatenate([s, bm], 1).astype(BF16)
                sb[c * 4 + h] = packed
                ab[c, h : h + 1, :] = jnp.broadcast_to(a, (1, 128))
                e_c = ee[c * 4 + h]
                m_c = e_c[:, 128:]
                p = dot(m_c.astype(BF16), packed)
                al = jnp.exp(cumt[c, h : h + 1, 127:128])
                s_cur[h] = al * s - p[:, :128] + e_c[:, :128]
                b_cur[h] = al * bm - a * m_c - p[:, 128:]
                a_cur[h] = a * al
        for h in heads:
            a_full = jnp.broadcast_to(a_cur[h], (16, 128))
            a_hi = a_full.astype(BF16).astype(F32)
            send[h, 0:128, :] = b_cur[h].T.astype(BF16)
            send[h, 128:256, :] = s_cur[h].T.astype(BF16)
            send[h, 256:272, :] = jnp.where(row16 < 8, a_hi, a_full - a_hi).astype(BF16)

    def to_line(z):
        return remote(send.at[z], recv.at[zz], msend.at[z], mrecv.at[zz], at_z(z))

    def total_to(y):
        return remote(tsend, trecv.at[yy], tsems.at[y], tsems.at[LINE + yy], at_y(y))

    def give(z):
        return remote(step_out.at[z], entering.at[zz], osend.at[z], orecv.at[zz], at_z(z))

    for c in range(NC):
        for g in range(2):
            systems(c, g)
    invert()
    for c in range(NC):
        for g in range(2):
            unit(c, g)
    map_of(range(HEADS))

    for z in range(LINE):
        @pl.when(z > zz)
        def _(z=z):
            pl.semaphore_wait(ready.at[z], 1)

        @pl.when((z != zz) & (chip < LAST))
        def _(z=z):
            to_line(z).start()

    recv[zz] = send[zz]

    def local_part(c, carry):
        r = chunk_rows(c)
        cc_all = cum[c]
        a_all = ab[c]
        for h in range(HEADS):
            g = h // 2
            q = qs[r, g * 128 : (g + 1) * 128].astype(F32)
            o = dot(att[c * 4 + h], uw[c * 4 + h])
            qeff = jnp.exp(cc_all[:, h : h + 1]) * q - o[:, 128:]
            rr = dot(qeff.astype(BF16), sb[c * 4 + h])
            outloc[r, h * 128 : (h + 1) * 128] = o[:, :128] + rr[:, :128]
            reach[r, h * 128 : (h + 1) * 128] = (a_all[h : h + 1, :] * qeff + rr[:, 128:]).astype(BF16)
        return carry

    run(local_part)

    def arrived(z):
        @pl.when(z != zz)
        def _():
            remote(send.at[0], recv.at[z], msend.at[0], mrecv.at[z], partner).wait_recv()

    def factor(rows):
        v = rows.astype(F32)
        return v[0:1, :] + v[8:9, :]

    def split(a):
        full = jnp.broadcast_to(a, (16, 128))
        hi = full.astype(BF16).astype(F32)
        return jnp.where(row16 < 8, hi, full - hi).astype(BF16)

    def follow(x, a, m):
        bt = recv[m, 0:128, :]
        a_m = factor(recv[m, 256:272, :])
        after = jnp.concatenate([a * bt.astype(F32), recv[m, 128:256, :].astype(F32)], 0)
        return a_m * x + dot(x.astype(BF16), bt) + after, a * a_m

    for z in range(LINE - 1):
        arrived(z)
    x = recv[0, 0:256, :].astype(F32)
    a = factor(recv[0, 256:272, :])
    for z in range(1, LINE):
        pre_x[z - 1] = x
        pre_a[z - 1, 0:1, :] = a
        if z < LINE - 1:
            x, a = follow(x, a, z)

    @pl.when(yy < LINE - 1)
    def _():
        arrived(LINE - 1)
        t, t_a = follow(pre_x[LINE - 2], pre_a[LINE - 2, 0:1, :], LINE - 1)
        tsend[0:256, :] = t.astype(BF16)
        tsend[256:272, :] = split(t_a)
        for y in range(1, LINE):
            @pl.when(y > yy)
            def _(y=y):
                pl.semaphore_wait(ready.at[LINE + y], 1)
                total_to(y).start()

    for b in range(2):
        w_copies[4 + b].wait()
    gain = jnp.concatenate([norm_gain[...].reshape(1, 128)] * 2, 1)

    def gate_rows(t, carry):
        r = chunk_rows(t)
        h_rows = hid[chunk_rows(t), :]
        for b in range(2):
            zs[r, b * 256 : (b + 1) * 256] = silu(dot(h_rows, wbuf[4 + b])) * gain
        return carry

    run(gate_rows)

    st_copy.wait()
    st0[...] = st0[...].T
    for y in range(LINE - 1):
        @pl.when(y < yy)
        def _(y=y):
            remote(tsend, trecv.at[y], tsems.at[0], tsems.at[LINE + y], partner).wait_recv()
            s = st0[...]
            st0[...] = (
                factor(trecv[y, 256:272, :]) * s
                + dot(s.astype(BF16), trecv[y, 0:128, :])
                + trecv[y, 128:256, :].astype(F32)
            )

    s_line = st0[...]
    s_bf = s_line.astype(BF16)
    step_out[0] = s_bf
    for z in range(1, LINE):
        step_out[z] = (
            pre_a[z - 1, 0:1, :] * s_line + dot(s_bf, pre_x[z - 1, 0:128, :].astype(BF16)) + pre_x[z - 1, 128:256, :]
        ).astype(BF16)
    for z in range(LINE):
        @pl.when(z != zz)
        def _(z=z):
            give(z).start()

    entering[zz] = step_out[zz]
    for z in range(LINE):
        @pl.when(z != zz)
        def _(z=z):
            remote(step_out.at[0], entering.at[z], osend.at[0], orecv.at[z], partner).wait_recv()

    def finish(side, x, put):
        r = pl.ds(pl.multiple_of(side * OWN + x * 64, 64), 64)
        rz = pl.ds(pl.multiple_of(lax.select(side == core, 0, OWN) + x * 64, 64), 64)
        for h in range(HEADS):
            cols = slice(h * 128, (h + 1) * 128)
            o = outloc[r, cols] + dot_nt(reach[r, cols], entering[h])
            n = o * lax.rsqrt(jnp.mean(o * o, axis=-1, keepdims=True) + 1e-6) * zs[rz, cols]
            put(cols, n.astype(BF16))

    def to_partner(i, x):
        def put(cols, v):
            nsend[i, :, cols] = v

        finish(other, x, put)

    def keep(i, x):
        def put(cols, v):
            nfull[core, i, :, cols] = v

        finish(core, x, put)

    def block(i, n0, width):
        cols = slice(n0, n0 + width)
        return dot(nfull[0, i], wo[0:512, cols]) + dot(nfull[1, i], wo[512:1024, cols])

    def fill(dst, i, n0):
        for j in range(2):
            dst[:, j * 512 : (j + 1) * 512] = block(i, n0 + j * 512, 512).astype(BF16)

    n_first = remote(nsend.at[0], nfull.at[core, 0], nsem.at[0], nsem.at[2], partner)
    n_rest = remote(nsend.at[pl.ds(1, 3)], nfull.at[core, pl.ds(1, 3)], nsem.at[1], nsem.at[3], partner)
    to_partner(0, across)
    n_first.start()
    keep(0, across)
    for i, x in ((1, right), (2, left), (3, xx)):
        to_partner(i, x)
    n_rest.start()
    wo_copy.wait()
    n_first.wait_recv()

    relay_r = remote(rs_send.at[0], rs_relay.at[0], rsend.at[0], rrecv.at[0], at_x(right))
    relay_l = remote(rs_send.at[1], rs_relay.at[1], rsend.at[1], rrecv.at[1], at_x(left))
    direct_r = remote(rs_send.at[2], rs_arr.at[0], rsend.at[2], rrecv.at[2], at_x(right))
    direct_l = remote(rs_send.at[3], rs_arr.at[1], rsend.at[3], rrecv.at[3], at_x(left))
    sum_r = remote(rs_send.at[4], rs_arr.at[2], rsend.at[4], rrecv.at[4], at_x(right))
    sum_l = remote(rs_send.at[5], rs_arr.at[3], rsend.at[5], rrecv.at[5], at_x(left))
    fill(rs_send.at[0], 0, 0)
    relay_r.start()
    fill(rs_send.at[1], 0, 1024)
    relay_l.start()
    for i, x in ((1, right), (2, left), (3, xx)):
        keep(i, x)
    n_rest.wait_recv()
    fill(rs_send.at[2], 1, 1024)
    direct_r.start()
    fill(rs_send.at[3], 2, 0)
    direct_l.start()
    for j in range(2):
        rs_hold[0, :, j * 512 : (j + 1) * 512] = block(1, j * 512, 512)
    for j in range(2):
        rs_hold[1, :, j * 512 : (j + 1) * 512] = block(2, 1024 + j * 512, 512)
    relay_r.wait_recv()
    rs_send[4] = (rs_hold[0] + rs_relay[0].astype(F32)).astype(BF16)
    sum_r.start()
    relay_l.wait_recv()
    rs_send[5] = (rs_hold[1] + rs_relay[1].astype(F32)).astype(BF16)
    sum_l.start()
    for j in range(4):
        rs_own[:, j * 512 : (j + 1) * 512] = block(3, j * 512, 512)
    direct_r.wait_recv()
    direct_l.wait_recv()
    sum_r.wait_recv()
    sum_l.wait_recv()
    out[:, 0:1024] = (rs_own[:, 0:1024] + rs_arr[1].astype(F32) + rs_arr[2].astype(F32)).astype(BF16)
    out[:, 1024:2048] = (rs_own[:, 1024:2048] + rs_arr[0].astype(F32) + rs_arr[3].astype(F32)).astype(BF16)

    for cp in swaps:
        cp.wait_send()

    @pl.when(sends_halo)
    def _():
        halo0.wait_send()
        halo1.wait_send()

    for n in range(LINE):
        @pl.when((n != zz) & (chip < LAST))
        def _(n=n):
            to_line(n).wait_send()

        @pl.when(n > yy)
        def _(n=n):
            total_to(n).wait_send()

        @pl.when(n != zz)
        def _(n=n):
            give(n).wait_send()

    n_first.wait_send()
    n_rest.wait_send()
    for cp in (relay_r, relay_l, direct_r, direct_l, sum_r, sum_l):
        cp.wait_send()


def on_device(*args):
    any_space = pl.BlockSpec(memory_space=pl.ANY)
    vmem = pl.BlockSpec(memory_space=pltpu.VMEM)
    smem = pl.BlockSpec(memory_space=pltpu.SMEM)
    dma = pltpu.SemaphoreType.DMA
    return pl.pallas_call(
        kernel,
        out_shape=jax.ShapeDtypeStruct((64, DM), BF16),
        in_specs=[any_space] * 5 + [vmem] * 5 + [smem] * 3 + [vmem] + [any_space] * 2,
        out_specs=vmem,
        scratch_shapes=[
            pltpu.VMEM((HALO + ROWS, DM), BF16),
            pltpu.VMEM((6, DM, 256), BF16),
            pltpu.VMEM((1024, DM), BF16),
            pltpu.VMEM((128, 128), F32),
            *[pltpu.VMEM((HALO + ROWS, 256), F32)] * 4,
            pltpu.VMEM((ROWS, 256), BF16),
            pltpu.VMEM((ROWS, 256), BF16),
            pltpu.VMEM((ROWS, 512), F32),
            pltpu.VMEM((ROWS, 512), F32),
            pltpu.VMEM((NC, CH, 128), F32),
            pltpu.VMEM((NC, 8, CH), F32),
            pltpu.VMEM((8, CH, 256), BF16),
            pltpu.VMEM((8, CH, 256), BF16),
            pltpu.VMEM((16, CH, CH), BF16),
            pltpu.VMEM((16, CH, 256), BF16),
            pltpu.VMEM((16, 128, 256), F32),
            pltpu.VMEM((16, 128, 256), BF16),
            pltpu.VMEM((NC, 8, 128), F32),
            pltpu.VMEM((ROWS, 512), BF16),
            pltpu.VMEM((ROWS, 512), F32),
            pltpu.VMEM((HEADS, MSG, 128), BF16),
            pltpu.VMEM((LINE, MSG, 128), BF16),
            pltpu.VMEM((MSG, 128), BF16),
            pltpu.VMEM((LINE, MSG, 128), BF16),
            pltpu.VMEM((LINE - 1, 256, 128), F32),
            pltpu.VMEM((LINE - 1, 8, 128), F32),
            pltpu.VMEM((LINE, 128, 128), BF16),
            pltpu.VMEM((HEADS, 128, 128), BF16),
            pltpu.VMEM((4, 64, 512), BF16),
            pltpu.VMEM((2, 4, 64, 512), BF16),
            pltpu.VMEM((6, 64, 1024), BF16),
            pltpu.VMEM((2, 64, 1024), BF16),
            pltpu.VMEM((4, 64, 1024), BF16),
            pltpu.VMEM((64, DM), F32),
            pltpu.VMEM((2, 64, 1024), F32),
            dma((5,)),
            dma((6,)),
            dma((8,)),
            dma((3,)),
            dma((HEADS,)),
            dma((LINE,)),
            dma((2 * LINE,)),
            dma((LINE,)),
            dma((LINE,)),
            dma((4,)),
            dma((6,)),
            dma((6,)),
            pltpu.SemaphoreType.REGULAR((2 * LINE,)),
        ],
        compiler_params=pltpu.CompilerParams(
            collective_id=0, has_side_effects=True, vmem_limit_bytes=56 * 1024 * 1024
        ),
    )(*args[:5], args[5].T, args[6].T, *args[7:])


def solution(mesh):
    placed = (
        P("seq", None),
        P(None, "head"),
        P(None, "head"),
        P(None, "head"),
        P(None, "head"),
        P(None, "head"),
        P(None, "head"),
        P(None, "head"),
        P(None, "head"),
        P(None, "head"),
        P("head"),
        P("head"),
        P("head"),
        P(),
        P("head", None),
        P("head", None, None),
    )
    return jax.shard_map(
        on_device, mesh=mesh, in_specs=placed, out_specs=P(("seq", "head"), None), check_vma=False
    )
```

time: 51 us -> 49.2 us (0.965)
  Pallas kernels: 48.8 us -> 47.1 us
    pallas_call x1, Pallas kernels: 48.8 us -> 47.1 us  [on_device(): pl.pallas_call(kernel, out_shape=jax.ShapeDtypeStruct((64, DM), BF16), in...]
where the time goes in v3:
time: 49.2 us; the launch traced here: 48.8 us
  Pallas kernels  47.1 us (96%)
  local copies, waits for them, and re-layouts  1.67 us (3%)
    pallas_call x1, Pallas kernels, on_device(): pl.pallas_call(kernel, out_shape=jax.ShapeDtypeStruct((64, DM), BF16), in...  47.1 us
    unnamed x1, local copies, waits for them, and re-layouts  1.67 us

profile of v3, /device:TPU:24, one launch (start us, length us, event | category | flops | bytes accessed | tf_op | source)
XLA Modules:
  0.0 48.8 jit_solution(2883692346640377780)
XLA Ops:
  0.0 47.1 %shard_map.154 = bf16[64,2048]{1,0:T(8,128)(2,1)} custom-call(bf16[256,2048]{1,0:T(8,128)(2,1)} %hidden.1, bf16[2048,512]{1,0:T(8,128)(2,1)} %w_query.1, bf16[2048,512]{1,0:T(8,128)(2,1)} %w_key.1, bf16[2048,1024]{1,0:T(8,128)(2,1)} %w_value.1, bf16[2048,1024]{1,0:T(8,128)(2,1)} %w_gate_z.1, bf16[8,2048]{1,0:T(8,128)(2,1)} %bitcast.2, ...), custom_call_target="tpu_custom_call" | custom-call | tf_op jit(solution)/shard_map/pallas_call | solution.py:567
  47.1 1.7 %copy.18 = bf16[64,2048]{1,0:T(8,128)(2,1)} copy(bf16[64,2048]{1,0:T(8,128)(2,1)} %shard_map.154) | data formatting | bytes 524288

commit v4 on v3

--- a/solution.py
+++ b/solution.py
@@ -331,6 +331,11 @@
     def total_to(y):
         return remote(tsend, trecv.at[yy], tsems.at[y], tsems.at[LINE + yy], at_y(y))
 
+    half = pl.ds(128, 128)
+
+    def state_to(y):
+        return remote(tsend.at[half], trecv.at[0, half], tsems.at[y], tsems.at[LINE], at_y(y))
+
     def give(z):
         return remote(step_out.at[z], entering.at[zz], osend.at[z], orecv.at[zz], at_z(z))
 
@@ -343,14 +348,15 @@
             unit(c, g)
     map_of(range(HEADS))
 
-    for z in range(LINE):
+    for z in range(1, LINE):
         @pl.when(z > zz)
         def _(z=z):
             pl.semaphore_wait(ready.at[z], 1)
 
-        @pl.when((z != zz) & (chip < LAST))
-        def _(z=z):
-            to_line(z).start()
+    @pl.when(chip < LAST)
+    def _():
+        for k in (2, 3, 1):
+            to_line(lax.rem(zz + k, LINE)).start()
 
     recv[zz] = send[zz]
 
@@ -390,6 +396,8 @@
         after = jnp.concatenate([a * bt.astype(F32), recv[m, 128:256, :].astype(F32)], 0)
         return a_m * x + dot(x.astype(BF16), bt) + after, a * a_m
 
+    st_copy.wait()
+    st0[...] = st0[...].T
     for z in range(LINE - 1):
         arrived(z)
     x = recv[0, 0:256, :].astype(F32)
@@ -404,13 +412,26 @@
     def _():
         arrived(LINE - 1)
         t, t_a = follow(pre_x[LINE - 2], pre_a[LINE - 2, 0:1, :], LINE - 1)
-        tsend[0:256, :] = t.astype(BF16)
-        tsend[256:272, :] = split(t_a)
         for y in range(1, LINE):
             @pl.when(y > yy)
             def _(y=y):
                 pl.semaphore_wait(ready.at[LINE + y], 1)
-                total_to(y).start()
+
+        @pl.when(yy == 0)
+        def _():
+            s = st0[...]
+            tsend[128:256, :] = (t_a * s + dot(s.astype(BF16), t[0:128].astype(BF16)) + t[128:256]).astype(BF16)
+            for y in range(1, LINE):
+                state_to(y).start()
+
+        @pl.when(yy > 0)
+        def _():
+            tsend[0:256, :] = t.astype(BF16)
+            tsend[256:272, :] = split(t_a)
+            for y in range(2, LINE):
+                @pl.when(y > yy)
+                def _(y=y):
+                    total_to(y).start()
 
     for b in range(2):
         w_copies[4 + b].wait()
@@ -425,9 +446,12 @@
 
     run(gate_rows)
 
-    st_copy.wait()
-    st0[...] = st0[...].T
-    for y in range(LINE - 1):
+    @pl.when(yy > 0)
+    def _():
+        remote(tsend.at[half], trecv.at[0, half], tsems.at[0], tsems.at[LINE], partner).wait_recv()
+        st0[...] = trecv[0, 128:256, :].astype(F32)
+
+    for y in range(1, LINE - 1):
         @pl.when(y < yy)
         def _(y=y):
             remote(tsend, trecv.at[y], tsems.at[0], tsems.at[LINE + y], partner).wait_recv()
@@ -445,11 +469,8 @@
         step_out[z] = (
             pre_a[z - 1, 0:1, :] * s_line + dot(s_bf, pre_x[z - 1, 0:128, :].astype(BF16)) + pre_x[z - 1, 128:256, :]
         ).astype(BF16)
-    for z in range(LINE):
-        @pl.when(z != zz)
-        def _(z=z):
-            give(z).start()
-
+    for k in (2, 3, 1):
+        give(lax.rem(zz + k, LINE)).start()
     entering[zz] = step_out[zz]
     for z in range(LINE):
         @pl.when(z != zz)
@@ -490,9 +511,7 @@
     to_partner(0, across)
     n_first.start()
     keep(0, across)
-    for i, x in ((1, right), (2, left), (3, xx)):
-        to_partner(i, x)
-    n_rest.start()
+    to_partner(1, right)
     wo_copy.wait()
     n_first.wait_recv()
 
@@ -506,6 +525,9 @@
     relay_r.start()
     fill(rs_send.at[1], 0, 1024)
     relay_l.start()
+    to_partner(2, left)
+    to_partner(3, xx)
+    n_rest.start()
     for i, x in ((1, right), (2, left), (3, xx)):
         keep(i, x)
     n_rest.wait_recv()
@@ -527,10 +549,12 @@
         rs_own[:, j * 512 : (j + 1) * 512] = block(3, j * 512, 512)
     direct_r.wait_recv()
     direct_l.wait_recv()
+    rs_own[:, 0:1024] += rs_arr[1].astype(F32)
+    rs_own[:, 1024:2048] += rs_arr[0].astype(F32)
     sum_r.wait_recv()
+    out[:, 0:1024] = (rs_own[:, 0:1024] + rs_arr[2].astype(F32)).astype(BF16)
     sum_l.wait_recv()
-    out[:, 0:1024] = (rs_own[:, 0:1024] + rs_arr[1].astype(F32) + rs_arr[2].astype(F32)).astype(BF16)
-    out[:, 1024:2048] = (rs_own[:, 1024:2048] + rs_arr[0].astype(F32) + rs_arr[3].astype(F32)).astype(BF16)
+    out[:, 1024:2048] = (rs_own[:, 1024:2048] + rs_arr[3].astype(F32)).astype(BF16)
 
     for cp in swaps:
         cp.wait_send()
@@ -545,9 +569,14 @@
         def _(n=n):
             to_line(n).wait_send()
 
-        @pl.when(n > yy)
+        @pl.when((n > yy) & (yy > 0))
         def _(n=n):
             total_to(n).wait_send()
+
+        if n > 0:
+            @pl.when(yy == 0)
+            def _(n=n):
+                state_to(n).wait_send()
 
         @pl.when(n != zz)
         def _(n=n):

time: 49.2 us -> 48.1 us (0.978)
  Pallas kernels: 47.1 us -> 46.2 us
    pallas_call x1, Pallas kernels: 47.1 us -> 46.2 us  [on_device(): pl.pallas_call(kernel, out_shape=jax.ShapeDtypeStruct((64, DM), BF16), in...]
where the time goes in v4:
time: 48.1 us; the launch traced here: 47.9 us
  Pallas kernels  46.2 us (96%)
  local copies, waits for them, and re-layouts  1.67 us (3%)
    pallas_call x1, Pallas kernels, on_device(): pl.pallas_call(kernel, out_shape=jax.ShapeDtypeStruct((64, DM), BF16), in...  46.2 us
    unnamed x1, local copies, waits for them, and re-layouts  1.67 us

profile of v4, /device:TPU:24, one launch (start us, length us, event | category | flops | bytes accessed | tf_op | source)
XLA Modules:
  0.0 47.9 jit_solution(2467765399196712196)
XLA Ops:
  0.0 46.2 %shard_map.154 = bf16[64,2048]{1,0:T(8,128)(2,1)} custom-call(bf16[256,2048]{1,0:T(8,128)(2,1)} %hidden.1, bf16[2048,512]{1,0:T(8,128)(2,1)} %w_query.1, bf16[2048,512]{1,0:T(8,128)(2,1)} %w_key.1, bf16[2048,1024]{1,0:T(8,128)(2,1)} %w_value.1, bf16[2048,1024]{1,0:T(8,128)(2,1)} %w_gate_z.1, bf16[8,2048]{1,0:T(8,128)(2,1)} %bitcast.2, ...), custom_call_target="tpu_custom_call" | custom-call | tf_op jit(solution)/shard_map/pallas_call | solution.py:596
  46.2 1.7 %copy.18 = bf16[64,2048]{1,0:T(8,128)(2,1)} copy(bf16[64,2048]{1,0:T(8,128)(2,1)} %shard_map.154) | data formatting | bytes 524288

commit v5 on v4

--- a/solution.py
+++ b/solution.py
@@ -277,7 +277,8 @@
                 tri[p] = (t_old.astype(F32) - y).astype(BF16)
             return size * 2
 
-        lax.fori_loop(0, 6, double, jnp.int32(2))
+        for level in range(6):
+            double(level, 2 << level)
 
     def unit(c, g):
         r = chunk_rows(c)

time: 48.1 us -> 46 us (0.956)
  Pallas kernels: 46.2 us -> 44.1 us
    pallas_call x1, Pallas kernels: 46.2 us -> 44.1 us  [on_device(): pl.pallas_call(kernel, out_shape=jax.ShapeDtypeStruct((64, DM), BF16), in...]
where the time goes in v5:
time: 46 us; the launch traced here: 45.8 us
  Pallas kernels  44.1 us (96%)
  local copies, waits for them, and re-layouts  1.67 us (4%)
    pallas_call x1, Pallas kernels, on_device(): pl.pallas_call(kernel, out_shape=jax.ShapeDtypeStruct((64, DM), BF16), in...  44.1 us
    unnamed x1, local copies, waits for them, and re-layouts  1.67 us

profile of v5, /device:TPU:24, one launch (start us, length us, event | category | flops | bytes accessed | tf_op | source)
XLA Modules:
  0.0 45.8 jit_solution(10168456306825467237)
XLA Ops:
  0.0 44.1 %shard_map.154 = bf16[64,2048]{1,0:T(8,128)(2,1)} custom-call(bf16[256,2048]{1,0:T(8,128)(2,1)} %hidden.1, bf16[2048,512]{1,0:T(8,128)(2,1)} %w_query.1, bf16[2048,512]{1,0:T(8,128)(2,1)} %w_key.1, bf16[2048,1024]{1,0:T(8,128)(2,1)} %w_value.1, bf16[2048,1024]{1,0:T(8,128)(2,1)} %w_gate_z.1, bf16[8,2048]{1,0:T(8,128)(2,1)} %bitcast.2, ...), custom_call_target="tpu_custom_call" | custom-call | tf_op jit(solution)/shard_map/pallas_call | solution.py:597
  44.1 1.7 %copy.18 = bf16[64,2048]{1,0:T(8,128)(2,1)} copy(bf16[64,2048]{1,0:T(8,128)(2,1)} %shard_map.154) | data formatting | bytes 524288

commit v6 on v5

--- a/solution.py
+++ b/solution.py
@@ -161,7 +161,13 @@
         cp.start()
     st_copy.start()
     wo_copy.start()
-    for cp in swaps:
+    for cp in swaps[:2]:
+        cp.wait_recv()
+    first_half = pl.ds(pl.multiple_of(HALO + other * OWN, 16), 128)
+    second_half = pl.ds(pl.multiple_of(HALO + other * OWN + 128, 16), 128)
+    for b in range(4):
+        raws[b][first_half, :] = dot(hid[OWN : OWN + 128, :], wbuf[b]).astype(BF16).astype(F32)
+    for cp in swaps[2:]:
         cp.wait_recv()
 
     @pl.when(chip > 0)
@@ -180,9 +186,9 @@
     )
     for b in range(4):
         raw = raws[b]
-        rest = dot(hid[OWN : ROWS + HALO, :], wbuf[b]).astype(BF16).astype(F32)
-        raw[rows_other, :] = rest[:OWN]
-        raw[0:HALO, :] = rest[OWN:]
+        rest = dot(hid[OWN + 128 : ROWS + HALO, :], wbuf[b]).astype(BF16).astype(F32)
+        raw[second_half, :] = rest[:128]
+        raw[0:HALO, :] = rest[128:]
         taps = taps_of[b]()
         for t in range(NC):
             pre = jnp.zeros((CH, 256), F32)
@@ -266,15 +272,14 @@
         pairs = range(2 * NC)
 
         def double(level, size):
-            mask = (pxor >= size) & (pxor < 2 * size)
+            mask = jnp.where((pxor >= size) & (pxor < 2 * size), 1.0, 0.0).astype(BF16)
             prods = []
             for p in pairs:
-                lm = jnp.where(mask, low[p].astype(F32), 0.0).astype(BF16)
+                lm = low[p] * mask
                 prods.append(dot(tri[p], pair_diag(lm)).astype(BF16))
             for p, prod in zip(pairs, prods):
                 t_old = tri[p]
-                y = dot(prod, pair_diag(t_old))
-                tri[p] = (t_old.astype(F32) - y).astype(BF16)
+                tri[p] = t_old - dot(prod, pair_diag(t_old)).astype(BF16)
             return size * 2
 
         for level in range(6):

time: 46 us -> 46.1 us (level)
  no operation moved by 1% of the time
where the time goes in v6:
time: 46.1 us; the launch traced here: 45.9 us
  Pallas kernels  44.2 us (96%)
  local copies, waits for them, and re-layouts  1.67 us (4%)
    pallas_call x1, Pallas kernels, on_device(): pl.pallas_call(kernel, out_shape=jax.ShapeDtypeStruct((64, DM), BF16), in...  44.2 us
    unnamed x1, local copies, waits for them, and re-layouts  1.67 us

profile of v6, /device:TPU:24, one launch (start us, length us, event | category | flops | bytes accessed | tf_op | source)
XLA Modules:
  0.0 45.9 jit_solution(11945684483957012977)
XLA Ops:
  0.0 44.2 %shard_map.154 = bf16[64,2048]{1,0:T(8,128)(2,1)} custom-call(bf16[256,2048]{1,0:T(8,128)(2,1)} %hidden.1, bf16[2048,512]{1,0:T(8,128)(2,1)} %w_query.1, bf16[2048,512]{1,0:T(8,128)(2,1)} %w_key.1, bf16[2048,1024]{1,0:T(8,128)(2,1)} %w_value.1, bf16[2048,1024]{1,0:T(8,128)(2,1)} %w_gate_z.1, bf16[8,2048]{1,0:T(8,128)(2,1)} %bitcast.2, ...), custom_call_target="tpu_custom_call" | custom-call | tf_op jit(solution)/shard_map/pallas_call | solution.py:602
  44.2 1.7 %copy.18 = bf16[64,2048]{1,0:T(8,128)(2,1)} copy(bf16[64,2048]{1,0:T(8,128)(2,1)} %shard_map.154) | data formatting | bytes 524288
